TPU v7x, 256 devices: a whole 4x4x8 slice. The times are simulated.
256 devices in a mesh: ctx: 32 (over y, z_hi, x), tp: 8 (over z_lo, core).
Axes of the slice: x: 4, y: 4, z: 8 (z_hi: 2, z_lo: 4; z = z_hi * 4 + z_lo), core: 2. Of those that a mesh axis runs over, the one named last changes fastest.
Arguments:
- queries: bfloat16 [2048, 16384], P('tp', 'ctx'), may hold values from -6 to 6
- key_branch: bfloat16 [2048, 16384], P('tp', 'ctx'), may hold values from -6 to 6
- value_branch: bfloat16 [2048, 16384], P('tp', 'ctx'), may hold values from -6 to 6
- filters: bfloat16 [256, 16384], P(None, 'ctx'), may hold values from -6 to 6
- cotangent: bfloat16 [2048, 16384], P('tp', 'ctx'), may hold values from -6 to 6
Outputs:
- grad_queries: bfloat16 [2048, 16384], P('tp', 'ctx')
- grad_keys: bfloat16 [2048, 16384], P('tp', 'ctx')
- grad_values: bfloat16 [2048, 16384], P('tp', 'ctx')
- grad_filters: bfloat16 [256, 16384], P(None, 'ctx')
All inputs are finite; a program needn't handle non-finite values.
Results may differ from a plain program's by a relative error of at most 0.024.
Values may be sent and summed in bfloat16 or wider, within the bound.
A program may use at most 64 MiB of HBM per device.

v0:
```python
import math

import jax
import jax.numpy as jnp
from jax import lax
from jax.sharding import PartitionSpec as P


def product(form, left, right):
    return jnp.einsum(
        form,
        left.astype(jnp.bfloat16),
        right.astype(jnp.bfloat16),
        preferred_element_type=jnp.float32,
    )


def angle_table(row_count, col_count, modulus):
    product_index = (
        jnp.arange(row_count, dtype=jnp.int32)[:, None]
        * jnp.arange(col_count, dtype=jnp.int32)[None, :]
        % modulus
    )
    theta = product_index.astype(jnp.float32) * (2.0 * math.pi / modulus)
    return (jnp.cos(theta), jnp.sin(theta))


def make_tables(half_outer, inner_len):
    outer_len = 2 * half_outer
    total_len = outer_len * inner_len
    cosine_outer, sine_outer = angle_table(half_outer, outer_len, outer_len)
    twist_cos, twist_sin = angle_table(outer_len, inner_len, total_len)
    cosine_inner, sine_inner = angle_table(inner_len, inner_len, inner_len)
    return (cosine_outer, sine_outer, twist_cos, twist_sin, cosine_inner, sine_inner)


def forward_spectrum(signal, tables):
    cosine_outer, sine_outer, twist_cos, twist_sin, cosine_inner, sine_inner = tables
    first_re = product("anb,ac->ncb", signal, cosine_outer)
    first_im = -product("anb,ac->ncb", signal, sine_outer)
    mid_re = first_re * twist_cos + first_im * twist_sin
    mid_im = first_im * twist_cos - first_re * twist_sin
    spec_re = product("ncb,bd->ncd", mid_re, cosine_inner) + product(
        "ncb,bd->ncd", mid_im, sine_inner
    )
    spec_im = product("ncb,bd->ncd", mid_im, cosine_inner) - product(
        "ncb,bd->ncd", mid_re, sine_inner
    )
    return (spec_re, spec_im)


def inverse_spectrum(spec_re, spec_im, tables):
    cosine_outer, sine_outer, twist_cos, twist_sin, cosine_inner, sine_inner = tables
    back_re = product("ncd,db->ncb", spec_re, cosine_inner) - product(
        "ncd,db->ncb", spec_im, sine_inner
    )
    back_im = product("ncd,db->ncb", spec_im, cosine_inner) + product(
        "ncd,db->ncb", spec_re, sine_inner
    )
    turn_re = back_re * twist_cos - back_im * twist_sin
    turn_im = back_im * twist_cos + back_re * twist_sin
    signal = product("ac,ncb->anb", cosine_outer, turn_re) - product(
        "ac,ncb->anb", sine_outer, turn_im
    )
    total_len = 2 * cosine_outer.shape[0] * cosine_inner.shape[0]
    return signal * (1.0 / total_len)


def conv_core(gated, grad_conv, filter_part):
    half_outer, item_count, inner_len = gated.shape
    tap_scale = 1.0 / math.sqrt(half_outer * inner_len)
    tables = make_tables(half_outer, inner_len)
    gate_re, gate_im = forward_spectrum(gated, tables)
    tap_re, tap_im = forward_spectrum(filter_part, tables)
    tap_re = tap_re * tap_scale
    tap_im = tap_im * tap_scale
    grad_re, grad_im = forward_spectrum(grad_conv, tables)
    conv_out = inverse_spectrum(
        gate_re * tap_re - gate_im * tap_im, gate_re * tap_im + gate_im * tap_re, tables
    )
    grad_gated = inverse_spectrum(
        tap_re * grad_re + tap_im * grad_im, tap_re * grad_im - tap_im * grad_re, tables
    )
    tap_terms = inverse_spectrum(
        gate_re * grad_re + gate_im * grad_im, gate_re * grad_im - gate_im * grad_re, tables
    )
    summed = lax.psum(tap_terms.astype(jnp.bfloat16), "tp").astype(jnp.float32)
    grad_filter = (summed * tap_scale).astype(jnp.bfloat16)
    return (conv_out, grad_gated, grad_filter)


def per_device(queries, key_branch, value_branch, filters, cotangent):
    groups = lax.axis_size("ctx")
    channel_count, token_count = queries.shape
    per_peer = channel_count // groups

    def split_rows(array):
        return array.reshape(groups, per_peer, token_count)

    def join_rows(array):
        return array.reshape(channel_count, array.shape[-1])

    gated = (key_branch.astype(jnp.float32) * value_branch.astype(jnp.float32)).astype(jnp.bfloat16)
    grad_conv = (cotangent.astype(jnp.float32) * queries.astype(jnp.float32)).astype(jnp.bfloat16)
    gated_part = lax.all_to_all(split_rows(gated), "ctx", split_axis=0, concat_axis=0, tiled=True)
    grad_part = lax.all_to_all(
        split_rows(grad_conv), "ctx", split_axis=0, concat_axis=0, tiled=True
    )
    filter_part = lax.all_to_all(
        split_rows(filters), "ctx", split_axis=0, concat_axis=0, tiled=True
    )
    conv_out, grad_gated, grad_filter = conv_core(gated_part, grad_part, filter_part)
    conv_low, grad_low, grad_filter = (
        lax.all_to_all(
            conv_out.astype(jnp.bfloat16), "ctx", split_axis=0, concat_axis=0, tiled=True
        ),
        lax.all_to_all(
            grad_gated.astype(jnp.bfloat16), "ctx", split_axis=0, concat_axis=0, tiled=True
        ),
        lax.all_to_all(grad_filter, "ctx", split_axis=0, concat_axis=0, tiled=True),
    )
    grad_filter = join_rows(grad_filter)
    conv_low = join_rows(conv_low).astype(jnp.float32)
    grad_low = join_rows(grad_low).astype(jnp.float32)
    grad_query = (cotangent.astype(jnp.float32) * conv_low).astype(jnp.bfloat16)
    grad_key = (grad_low * value_branch.astype(jnp.float32)).astype(jnp.bfloat16)
    grad_value = (grad_low * key_branch.astype(jnp.float32)).astype(jnp.bfloat16)
    return (grad_query, grad_key, grad_value, grad_filter)


def solution(mesh):
    placed = (P("tp", "ctx"), P("tp", "ctx"), P("tp", "ctx"), P(None, "ctx"), P("tp", "ctx"))
    return jax.shard_map(
        per_device,
        mesh=mesh,
        in_specs=placed,
        out_specs=(P("tp", "ctx"), P("tp", "ctx"), P("tp", "ctx"), P(None, "ctx")),
        check_vma=False,
    )
```

profile of v0, /device:TPU:1, one launch (start us, length us, event | category | flops | bytes accessed | tf_op | source)
XLA Modules:
  0.0 326.1 jit_solution(3993386339746717331)
XLA Ops:
  9.0 14.6 %all-to-all-start.3 = ((bf16[32,8,512]{2,1,0:T(8,128)(2,1)}), bf16[32,8,512]{2,1,0:T(8,128)(2,1)S(1)}, u32[]{:S(2)}, u32[]{:S(2)}) async-start(bf16[32,8,512]{2,1,0:T(8,128)(2,1)} %fusion.79), calls=%async_computation.3 | async-start | bytes 524288 | tf_op jit(solution)/shard_map/all_to_all | solution.py:106
  24.9 10.8 %all-to-all-done.3 = bf16[32,8,512]{2,1,0:T(8,128)(2,1)S(1)} async-done(((bf16[32,8,512]{2,1,0:T(8,128)(2,1)}), bf16[32,8,512]{2,1,0:T(8,128)(2,1)S(1)}, u32[]{:S(2)}, u32[]{:S(2)}) %all-to-all-start.3) | async-done | bytes 262176 | tf_op jit(solution)/shard_map/all_to_all | solution.py:106
  40.4 11.1 %all-to-all-done.1 = bf16[32,8,512]{2,1,0:T(8,128)(2,1)S(1)} async-done(((bf16[32,8,512]{2,1,0:T(8,128)(2,1)}), bf16[32,8,512]{2,1,0:T(8,128)(2,1)S(1)}, u32[]{:S(2)}, u32[]{:S(2)}) %all-to-all-start.1) | async-done | bytes 262176 | tf_op jit(solution)/shard_map/all_to_all | solution.py:109
  59.9 9.0 %all-to-all-done = bf16[32,8,512]{2,1,0:T(8,128)(2,1)} async-done(((bf16[32,8,512]{2,1,0:T(8,128)(2,1)}), bf16[32,8,512]{2,1,0:T(8,128)(2,1)}, u32[]{:S(2)}, u32[]{:S(2)}) %all-to-all-start) | async-done | bytes 262176 | tf_op jit(solution)/shard_map/all_to_all | solution.py:105
  82.1 5.1 %convolution_subtract_fusion.2 = f32[8,64,512]{2,1,0:T(8,128)S(1)} fusion(f32[8,64,512]{2,1,0:T(8,128)S(1)} %fusion.62, bf16[8,64,512]{2,1,0:T(8,128)(2,1)S(1)} %get-tuple-element.11), kind=kOutput, calls=%fused_computation.7 | convolution fusion | flops 272629760 | bytes 2621440 | tf_op jit(solution)/shard_map/ncb,bd->ncd/dot_general | solution.py:10
  87.2 5.1 %convolution_add_fusion.2 = f32[8,64,512]{2,1,0:T(8,128)S(1)} fusion(f32[8,64,512]{2,1,0:T(8,128)S(1)} %fusion.64, bf16[8,64,512]{2,1,0:T(8,128)(2,1)S(1)} %get-tuple-element.10), kind=kOutput, calls=%fused_computation.8 | convolution fusion | flops 272629760 | bytes 2621440 | tf_op jit(solution)/shard_map/ncb,bd->ncd/dot_general | solution.py:10
  92.2 5.2 %fusion.74 = f32[8,64,512]{2,1,0:T(8,128)S(1)} fusion(bf16[8,64,512]{2,1,0:T(8,128)(2,1)S(1)} %get-tuple-element.22), kind=kOutput, calls=%fused_computation.99 | convolution fusion | flops 272367616 | bytes 1572864 | tf_op jit(solution)/shard_map/ncb,bd->ncd/dot_general | solution.py:10
  102.3 5.1 %fusion.1 = f32[8,64,512]{2,1,0:T(8,128)S(1)} fusion(f32[8,64,512]{2,1,0:T(8,128)S(1)} %fusion.74, bf16[8,64,512]{2,1,0:T(8,128)(2,1)S(1)} %get-tuple-element.23), kind=kOutput, calls=%fused_computation.16 | convolution fusion | flops 272891904 | bytes 2621440 | tf_op jit(solution)/shard_map/ncb,bd->ncd/dot_general | solution.py:10
  107.4 5.1 %fusion = f32[8,64,512]{2,1,0:T(8,128)S(1)} fusion(f32[8,64,512]{2,1,0:T(8,128)S(1)} %fusion.70, bf16[8,64,512]{2,1,0:T(8,128)(2,1)S(1)} %get-tuple-element.22), kind=kOutput, calls=%fused_computation.13 | convolution fusion | flops 272891904 | bytes 2621440 | tf_op jit(solution)/shard_map/ncb,bd->ncd/dot_general | solution.py:10
  117.4 5.0 %fusion.76 = f32[8,64,512]{2,1,0:T(8,128)S(1)} fusion(bf16[8,64,512]{2,1,0:T(8,128)(2,1)S(1)} %get-tuple-element.25), kind=kOutput, calls=%fused_computation.100 | convolution fusion | flops 272367616 | bytes 1572864 | tf_op jit(solution)/shard_map/ncb,bd->ncd/dot_general | solution.py:10
  122.4 5.1 %convolution_add_fusion.5 = f32[8,64,512]{2,1,0:T(8,128)S(1)} fusion(f32[8,64,512]{2,1,0:T(8,128)S(1)} %fusion.76, bf16[8,64,512]{2,1,0:T(8,128)(2,1)S(1)} %get-tuple-element.24), kind=kOutput, calls=%fused_computation.18 | convolution fusion | flops 272629760 | bytes 2621440 | tf_op jit(solution)/shard_map/ncb,bd->ncd/dot_general | solution.py:10
  127.5 5.6 %add_convert_fusion.1 = (bf16[8,64,512]{2,1,0:T(8,128)(2,1)S(1)}, bf16[8,64,512]{2,1,0:T(8,128)(2,1)S(1)}, bf16[8,64,512]{2,1,0:T(8,128)(2,1)S(1)}, bf16[8,64,51...) fusion(f32[8,64,512]{2,1,0:T(8,128)S(1)} %convolution_subtract_fusion.2, ...), kind=kOutput, calls=%fused_computation.35 | convolution fusion | flops 278921216 | bytes 9961472 | tf_op jit(solution)/shard_map/ncb,bd->ncd/dot_general | solution.py:10
  137.9 5.7 %fusion.54 = f32[8,64,512]{2,1,0:T(8,128)} fusion(bf16[8,64,512]{2,1,0:T(8,128)(2,1)S(1)} %get-tuple-element.5), kind=kOutput, calls=%fused_computation.89 | convolution fusion | flops 272367616 | bytes 1572864 | tf_op jit(solution)/shard_map/ncd,db->ncb/dot_general | solution.py:10
  143.6 5.0 %convolution_subtract_fusion = f32[8,64,512]{2,1,0:T(8,128)S(1)} fusion(f32[8,64,512]{2,1,0:T(8,128)S(1)} %fusion.56, bf16[8,64,512]{2,1,0:T(8,128)(2,1)S(1)} %get-tuple-element.5), kind=kOutput, calls=%fused_computation.4 | convolution fusion | flops 272629760 | bytes 2621440 | tf_op jit(solution)/shard_map/ncd,db->ncb/dot_general | solution.py:10
  148.6 5.0 %fusion.58 = f32[8,64,512]{2,1,0:T(8,128)S(1)} fusion(bf16[8,64,512]{2,1,0:T(8,128)(2,1)S(1)} %get-tuple-element.16), kind=kOutput, calls=%fused_computation.91 | convolution fusion | flops 272367616 | bytes 1572864 | tf_op jit(solution)/shard_map/ncd,db->ncb/dot_general | solution.py:10
  158.5 5.1 %convolution_add_fusion.1 = f32[8,64,512]{2,1,0:T(8,128)S(1)} fusion(f32[8,64,512]{2,1,0:T(8,128)S(1)} %fusion.58, bf16[8,64,512]{2,1,0:T(8,128)(2,1)S(1)} %get-tuple-element.17), kind=kOutput, calls=%fused_computation.5 | convolution fusion | flops 272629760 | bytes 2621440 | tf_op jit(solution)/shard_map/ncd,db->ncb/dot_general | solution.py:10
  163.6 5.1 %convolution_subtract_fusion.1 = f32[8,64,512]{2,1,0:T(8,128)S(1)} fusion(f32[8,64,512]{2,1,0:T(8,128)S(1)} %fusion.60, bf16[8,64,512]{2,1,0:T(8,128)(2,1)S(1)} %get-tuple-element.16), kind=kOutput, calls=%fused_computation.6 | convolution fusion | flops 272629760 | bytes 2621440 | tf_op jit(solution)/shard_map/ncd,db->ncb/dot_general | solution.py:10
  184.2 5.1 %convolution_add_fusion.3 = f32[8,64,512]{2,1,0:T(8,128)S(1)} fusion(f32[8,64,512]{2,1,0:T(8,128)S(1)} %fusion.66, bf16[8,64,512]{2,1,0:T(8,128)(2,1)S(1)} %get-tuple-element.19), kind=kOutput, calls=%fused_computation.10 | convolution fusion | flops 272629760 | bytes 2621440 | tf_op jit(solution)/shard_map/ncd,db->ncb/dot_general | solution.py:10
  189.2 5.1 %convolution_subtract_fusion.3 = f32[8,64,512]{2,1,0:T(8,128)S(1)} fusion(f32[8,64,512]{2,1,0:T(8,128)S(1)} %fusion.68, bf16[8,64,512]{2,1,0:T(8,128)(2,1)S(1)} %get-tuple-element.18), kind=kOutput, calls=%fused_computation.11 | convolution fusion | flops 272629760 | bytes 2621440 | tf_op jit(solution)/shard_map/ncd,db->ncb/dot_general | solution.py:10
  195.9 5.0 %convolution_add_fusion = f32[8,64,512]{2,1,0:T(8,128)S(1)} fusion(f32[8,64,512]{2,1,0:T(8,128)S(1)} %copy-done.8, bf16[8,64,512]{2,1,0:T(8,128)(2,1)S(1)} %get-tuple-element.4), kind=kOutput, calls=%fused_computation.3 | convolution fusion | flops 272629760 | bytes 2621440 | tf_op jit(solution)/shard_map/ncd,db->ncb/dot_general | solution.py:10
  201.3 11.8 %all-to-all-start.2 = ((bf16[32,8,512]{2,1,0:T(8,128)(2,1)}), bf16[32,8,512]{2,1,0:T(8,128)(2,1)S(1)}, u32[]{:S(2)}, u32[]{:S(2)}) async-start(bf16[32,8,512]{2,1,0:T(8,128)(2,1)} %copy.19), calls=%async_computation.2 | async-start | bytes 524288 | tf_op jit(solution)/shard_map/all_to_all | solution.py:114
  214.2 78.5 %all-reduce.2.cloned.1.call-done = bf16[32,8,512]{2,0,1:T(8,128)(2,1)} async-done(((bf16[32,8,512]{2,0,1:T(8,128)(2,1)}), bf16[32,8,512]{2,0,1:T(8,128)(2,1)}) %all-reduce.2.cloned.1.call-update) | async-done | bytes 262160 | tf_op jit(solution)/shard_map/psum | solution.py:87
  294.5 11.5 %all-to-all-start.5 = ((bf16[32,8,512]{2,1,0:T(8,128)(2,1)}), bf16[32,8,512]{2,1,0:T(8,128)(2,1)S(1)}, u32[]{:S(2)}, u32[]{:S(2)}) async-start(bf16[32,8,512]{2,1,0:T(8,128)(2,1)} %copy.23), calls=%async_computation.5 | async-start | bytes 524288 | tf_op jit(solution)/shard_map/all_to_all | solution.py:120
  308.0 10.0 %all-to-all-done.5 = bf16[32,8,512]{2,1,0:T(8,128)(2,1)S(1)} async-done(((bf16[32,8,512]{2,1,0:T(8,128)(2,1)}), bf16[32,8,512]{2,1,0:T(8,128)(2,1)S(1)}, u32[]{:S(2)}, u32[]{:S(2)}) %all-to-all-start.5) | async-done | bytes 262176 | tf_op jit(solution)/shard_map/all_to_all | solution.py:120
  (55 shorter events, 71.8 us)
Async XLA Ops:
  9.0 15.2 %copy-start.4 = (bf16[256,512]{1,0:T(8,128)(2,1)S(1)}, bf16[256,512]{1,0:T(8,128)(2,1)}, u32[]{:S(2)}) copy-start(bf16[256,512]{1,0:T(8,128)(2,1)} %param.7) | copy-start | bytes 786436
  9.0 15.2 %copy-start.6 = (bf16[256,512]{1,0:T(8,128)(2,1)S(1)}, bf16[256,512]{1,0:T(8,128)(2,1)}, u32[]{:S(2)}) copy-start(bf16[256,512]{1,0:T(8,128)(2,1)} %param.6) | copy-start | bytes 786436
  9.0 26.7 %all-to-all-start.3 = ((bf16[32,8,512]{2,1,0:T(8,128)(2,1)}), bf16[32,8,512]{2,1,0:T(8,128)(2,1)S(1)}, u32[]{:S(2)}, u32[]{:S(2)}) async-start(bf16[32,8,512]{2,1,0:T(8,128)(2,1)} %fusion.79), calls=%async_computation.3 | async-start | bytes 524288 | tf_op jit(solution)/shard_map/all_to_all | solution.py:106
  35.7 15.8 %all-to-all-start.1 = ((bf16[32,8,512]{2,1,0:T(8,128)(2,1)}), bf16[32,8,512]{2,1,0:T(8,128)(2,1)S(1)}, u32[]{:S(2)}, u32[]{:S(2)}) async-start(bf16[32,8,512]{2,1,0:T(8,128)(2,1)} %bitcast.7), calls=%async_computation.1 | async-start | bytes 524288 | tf_op jit(solution)/shard_map/all_to_all | solution.py:109
  51.5 0.7 copy-start.1
  52.2 16.7 %all-to-all-start = ((bf16[32,8,512]{2,1,0:T(8,128)(2,1)}), bf16[32,8,512]{2,1,0:T(8,128)(2,1)}, u32[]{:S(2)}, u32[]{:S(2)}) async-start(bf16[32,8,512]{2,1,0:T(8,128)(2,1)} %fusion.78), calls=%async_computation | async-start | bytes 524288 | tf_op jit(solution)/shard_map/all_to_all | solution.py:105
  57.1 1.4 copy-start.2
  68.9 1.5 copy-start
  170.2 31.1 %all-to-all-start.4 = ((bf16[32,8,512]{2,1,0:T(8,128)(2,1)}), bf16[32,8,512]{2,1,0:T(8,128)(2,1)S(1)}, u32[]{:S(2)}, u32[]{:S(2)}) async-start(bf16[32,8,512]{2,1,0:T(8,128)(2,1)} %copy.22), calls=%async_computation.4 | async-start | bytes 524288 | tf_op jit(solution)/shard_map/all_to_all | solution.py:117
  194.6 1.2 copy-start.8
  201.3 93.3 %all-to-all-start.2 = ((bf16[32,8,512]{2,1,0:T(8,128)(2,1)}), bf16[32,8,512]{2,1,0:T(8,128)(2,1)S(1)}, u32[]{:S(2)}, u32[]{:S(2)}) async-start(bf16[32,8,512]{2,1,0:T(8,128)(2,1)} %copy.19), calls=%async_computation.2 | async-start | bytes 524288 | tf_op jit(solution)/shard_map/all_to_all | solution.py:114
  213.0 79.6 %all-reduce.2.cloned.1.call-start = ((), (), s32[]{:S(2)}) async-start(), calls=%async_computation.6 | async-start | bytes 524288 | tf_op jit(solution)/shard_map/psum | solution.py:87
  294.5 11.5 %copy-start.3 = (bf16[256,512]{1,0:T(8,128)(2,1)S(1)}, bf16[256,512]{1,0:T(8,128)(2,1)}, u32[]{:S(2)}) copy-start(bf16[256,512]{1,0:T(8,128)(2,1)} %param.9) | copy-start | bytes 786436
  294.5 23.6 %all-to-all-start.5 = ((bf16[32,8,512]{2,1,0:T(8,128)(2,1)}), bf16[32,8,512]{2,1,0:T(8,128)(2,1)S(1)}, u32[]{:S(2)}, u32[]{:S(2)}) async-start(bf16[32,8,512]{2,1,0:T(8,128)(2,1)} %copy.23), calls=%async_computation.5 | async-start | bytes 524288 | tf_op jit(solution)/shard_map/all_to_all | solution.py:120
  306.0 1.0 copy-start.5
  306.0 1.1 copy-start.7
Sparse Core Ops, SparseCore 0:
  217.1 75.5 all-reduce.1
where the time goes:
time: 330 us; the launch traced here: 326 us
  matrix products  131 us (40%)
  waiting for transfers between devices  119 us (36%)
  starting transfers between devices  50.8 us (15%)
  between operations  14.8 us (4%)
  other arithmetic  5.76 us (2%)
  local copies, waits for them, and re-layouts  4.33 us (1%)
    dot_general x36, matrix products, product(): jnp.einsum(form, left.astype(jnp.bfloat16), right.astype(jnp.bfloat16), p...  131 us
    psum x1, waiting for transfers between devices, conv_core(): summed = lax.psum(tap_terms.astype(jnp.bfloat16), 'tp').astype(jnp.float32)  78.5 us
    all_to_all x1, starting transfers between devices, per_device(): lax.all_to_all(split_rows(grad_conv), 'ctx', split_axis=0, concat_axis=0,...  14.6 us
    all_to_all x1, starting transfers between devices, per_device(): lax.all_to_all(conv_out.astype(jnp.bfloat16), 'ctx', split_axis=0, concat...  11.8 us
    all_to_all x1, starting transfers between devices, per_device(): lax.all_to_all(grad_filter, 'ctx', split_axis=0, concat_axis=0, tiled=True)  11.5 us
    all_to_all x1, waiting for transfers between devices, per_device(): lax.all_to_all(split_rows(filters), 'ctx', split_axis=0, concat_axis=0, t...  11.1 us
    all_to_all x1, waiting for transfers between devices, per_device(): lax.all_to_all(split_rows(grad_conv), 'ctx', split_axis=0, concat_axis=0,...  10.8 us
    all_to_all x1, waiting for transfers between devices, per_device(): lax.all_to_all(grad_filter, 'ctx', split_axis=0, concat_axis=0, tiled=True)  10 us
  transfers between devices with their start and end apart: 7, of which 5 were waited for; matrix products, arithmetic and copies ran while one was open for 11% of the time, Pallas kernels for 0%

commit v1 on v0

v1 whole, which is shorter than its diff:
```python
import functools

import jax
import jax.numpy as jnp
import ml_dtypes
import numpy as np
from jax import lax
from jax.experimental import pallas as pl
from jax.experimental.pallas import tpu as pltpu
from jax.sharding import PartitionSpec as P

MESH = pl.DeviceIdType.MESH
F32 = jnp.float32
BF16 = jnp.bfloat16

SEQ = 16384
CTX = 32
TP = 8
TOK = SEQ // CTX
R = 128
Q = TOK // R
SCALE = 2.0**-21


def tables():
    k = np.arange(R, dtype=np.float64)[:, None]
    n = np.arange(R, dtype=np.float64)[None, :]
    angle = 2 * np.pi * (k + 0.25) * n / R
    outer = np.concatenate([np.cos(angle), -np.sin(angle)], 0)
    order = np.arange(R).reshape(CTX, Q).T.reshape(-1)
    twist = 2 * np.pi * (k + 0.25) * n / SEQ
    inner = 2 * np.pi * ((k * n) % R) / R
    c, s = np.cos(inner), np.sin(inner)
    fwd = np.block([[c, -s], [s, c]])
    as_bf16 = lambda t: np.asarray(t, np.float32).astype(ml_dtypes.bfloat16)
    return (
        as_bf16(outer[:, order]),
        np.stack([np.cos(twist), np.sin(twist)]).astype(np.float32),
        as_bf16(fwd),
        as_bf16(fwd.T),
        as_bf16(outer.T[order]),
        as_bf16(outer.T),
    )


def dot(a, b):
    return jnp.dot(a, b, preferred_element_type=F32)


def exchange_kernel(
    q_ref, k_ref, v_ref, f_ref, c_ref, e1, tw, fw, fi, e1q, e1n,
    out_ref, fil_ref,
    snd, rcv, osnd, orcv, fs, fsnd, fall, sbuf, sf, spec, hspec, ytap, tarcv, tbsnd, tbrcv, tbown,
    csnd, crcv, cflat, dbuf,
    s_in, r_in, s_f, r_f, s_out, r_out, s_c, r_c, s_z, r_z, s_d, r_d, s_x, r_x,
):
    me = lax.axis_index("ctx")
    tp = lax.axis_index("tp")
    core = tp % 2
    zlo = tp // 2
    mx, mz, my = me % 4, (me // 4) % 2, me // 8
    mate = zlo * 2 + 1 - core

    def peer(i):
        dz = 1 - i // 16
        return ((my + (i // 4) % 4) % 4) * 8 + ((mz + dz) % 2) * 4 + (mx + i % 4) % 4

    def others(body):
        lax.fori_loop(0, 16, lambda i, _: (body(i), 0)[1], 0)
        lax.fori_loop(17, 32, lambda i, _: (body(i), 0)[1], 0)

    def chip(dz):
        return ((zlo + dz) % 4) * 2 + core

    def remote(src, dst, ss, rs, c, t):
        return pltpu.make_async_remote_copy(
            src_ref=src, dst_ref=dst, send_sem=ss, recv_sem=rs, device_id=(c, t), device_id_type=MESH)

    barrier = pltpu.get_barrier_semaphore()

    def greet(c, t):
        pl.semaphore_signal(barrier, inc=1, device_id=(c, t), device_id_type=MESH)

    others(lambda i: greet(peer(i), tp))
    greet(me, mate)
    for dz in (1, 2, 3):
        greet(me, chip(dz))

    def gates(j, _):
        rows = pl.ds(pl.multiple_of(j * 16, 16), 16)
        g = k_ref[rows, :].astype(F32) * v_ref[rows, :].astype(F32)
        d = c_ref[rows, :].astype(F32) * q_ref[rows, :].astype(F32)
        snd[2 * j] = jnp.concatenate([g[:8], d[:8]], 0).astype(BF16)
        snd[2 * j + 1] = jnp.concatenate([g[8:], d[8:]], 0).astype(BF16)
        return 0

    lax.fori_loop(0, CTX // 2, gates, 0)
    rcv[me] = snd[me]
    pl.semaphore_wait(barrier, 35)

    def in_copy(i):
        c = peer(i)
        return remote(snd.at[c], rcv.at[me], s_in.at[i], r_in.at[i], c, tp)

    others(lambda i: in_copy(i).start())

    for q in range(Q):
        fs[q] = f_ref[:, q * R:(q + 1) * R].astype(F32)
    for q in range(Q):
        for f in range(4):
            sf[0, pl.ds(q * 4 + f, CTX, stride=16), :] = fs[q, pl.ds(core * 4 + f, CTX, stride=8), :]
    for c in range(CTX):
        fsnd[c] = sf[0, c * 16:(c + 1) * 16, :].astype(BF16)
    fall[core, me] = fsnd[me]

    def f_copy(i):
        c = peer(i)
        return remote(fsnd.at[c], fall.at[core, me], s_f.at[i], r_f.at[i], c, tp)

    others(lambda i: f_copy(i).start())

    def forward(x):
        y = dot(e1[...], x)
        yr, yi = y[:R], y[R:]
        tc, ts = tw[0], tw[1]
        left = jnp.concatenate([(yr * tc + yi * ts).astype(BF16), (yi * tc - yr * ts).astype(BF16)], 1)
        return dot(left, fw[...])

    def inverse(pr, pi, out):
        u = dot(jnp.concatenate([pr.astype(BF16), pi.astype(BF16)], 1), fi[...])
        ur, ui = u[:, :R], u[:, R:]
        tc, ts = tw[0], tw[1]
        v = jnp.concatenate([(ur * tc - ui * ts).astype(BF16), (ui * tc + ur * ts).astype(BF16)], 0)
        return dot(out[...], v)

    others(lambda i: in_copy(i).wait_recv())

    def widen(c, _):
        v = rcv[c].astype(F32)
        for q in range(Q):
            sbuf[q, pl.ds(pl.multiple_of(c * 16, 16), 16), :] = v[:, q * R:(q + 1) * R]
        return 0

    lax.fori_loop(0, CTX, widen, 0)
    for r in range(16):
        x = jnp.concatenate([sbuf[q, pl.ds(r, CTX, stride=16), :] for q in range(Q)], 0)
        spec[r] = forward(x.astype(BF16))

    others(lambda i: f_copy(i).wait_recv())
    mate_f = remote(fall.at[core], fall.at[core], s_x.at[0], r_x.at[0], me, mate)
    mate_f.start()

    def tap(ch, _):
        g, d = spec[ch], spec[ch + 8]
        gr, gi, dr, di = g[:, :R], g[:, R:], d[:, :R], d[:, R:]
        ytap[ch] = inverse(gr * dr + gi * di, gr * di - gi * dr, e1n)
        return 0

    lax.fori_loop(0, 8, tap, 0)
    mate_t = remote(ytap.at[pl.ds((1 - core) * 4, 4)], tarcv, s_x.at[1], r_x.at[1], me, mate)
    mate_t.start()

    mate_f.wait_recv()
    for j in range(2):
        for c in range(CTX):
            sf[j, c * 16:(c + 1) * 16, :] = fall[j, c].astype(F32)
    for j in range(2):
        for f in range(4):
            x = jnp.concatenate([sf[j, pl.ds(q * 4 + f, CTX, stride=16), :] for q in range(Q)], 0)
            hspec[j * 4 + f] = forward(x.astype(BF16))

    mate_t.wait_recv()
    for f in range(4):
        tbsnd[f] = (ytap[core * 4 + f] + tarcv[f]).astype(BF16)

    def z_copy(dz):
        to = (zlo + dz) % 4
        return remote(tbsnd.at[to], tbrcv.at[dz], s_z.at[dz], r_z.at[dz], me, chip(dz))

    for dz in (1, 2, 3):
        z_copy(dz).start()
    tbown[...] = ytap[core * 4 + zlo] + tarcv[zlo]

    def place(r, y):
        for q in range(Q):
            sbuf[q, pl.ds(r, CTX, stride=16), :] = y[q * CTX:(q + 1) * CTX]

    for ch in range(8):
        g, h = spec[ch], hspec[ch]
        gr, gi, hr, hi = g[:, :R], g[:, R:], h[:, :R], h[:, R:]
        place(ch, inverse(gr * hr - gi * hi, gr * hi + gi * hr, e1q))
    for ch in range(8):
        d, h = spec[ch + 8], hspec[ch]
        dr, di, hr, hi = d[:, :R], d[:, R:], h[:, :R], h[:, R:]
        place(ch + 8, inverse(hr * dr + hi * di, hr * di - hi * dr, e1q))

    def narrow(c, _):
        rows = pl.ds(pl.multiple_of(c * 16, 16), 16)
        v = jnp.concatenate([sbuf[q, rows, :] for q in range(Q)], 1)
        osnd[c] = (v * SCALE).astype(BF16)
        return 0

    lax.fori_loop(0, CTX, narrow, 0)
    orcv[me] = osnd[me]

    def out_copy(i):
        c = peer(i)
        return remote(osnd.at[c], orcv.at[me], s_out.at[i], r_out.at[i], c, tp)

    others(lambda i: out_copy(i).start())

    for dz in (1, 2, 3):
        z_copy(dz).wait_recv()
    total = (tbown[...] + tbrcv[1].astype(F32) + tbrcv[2].astype(F32) + tbrcv[3].astype(F32)) * SCALE
    for c in range(CTX):
        csnd[c] = total[c * Q:(c + 1) * Q]
    crcv[me] = csnd[me]

    def c_copy(i):
        c = peer(i)
        return remote(csnd.at[c], crcv.at[me], s_c.at[i], r_c.at[i], c, tp)

    others(lambda i: c_copy(i).start())
    others(lambda i: c_copy(i).wait_recv())
    for c in range(CTX):
        cflat[c * Q:(c + 1) * Q, :] = crcv[c]
    dbuf[core, zlo] = jnp.concatenate([cflat[pl.ds(q, CTX, stride=Q), :] for q in range(Q)], 0).astype(BF16)

    def d_copy(dz):
        return remote(dbuf.at[core, zlo], dbuf.at[core, zlo], s_d.at[dz], r_d.at[dz], me, chip(dz))

    for dz in (1, 2, 3):
        d_copy(dz).start()
    for dz in (1, 2, 3):
        d_copy(dz).wait_recv()
    mate_d = remote(dbuf.at[core], dbuf.at[core], s_x.at[2], r_x.at[2], me, mate)
    mate_d.start()

    others(lambda i: out_copy(i).wait_recv())
    out_ref[...] = orcv[...]
    mate_d.wait_recv()
    fil_ref[...] = dbuf[...]

    others(lambda i: in_copy(i).wait_send())
    others(lambda i: f_copy(i).wait_send())
    others(lambda i: out_copy(i).wait_send())
    others(lambda i: c_copy(i).wait_send())
    for dz in (1, 2, 3):
        z_copy(dz).wait_send()
        d_copy(dz).wait_send()
    mate_f.wait_send()
    mate_t.wait_send()
    mate_d.wait_send()


def finish_kernel(o_ref, d_ref, c_ref, k_ref, v_ref, gq_ref, gk_ref, gv_ref, gf_ref, wide):
    def gates(j, _):
        rows = pl.ds(pl.multiple_of(j * 16, 16), 16)
        a, b = o_ref[2 * j].astype(F32), o_ref[2 * j + 1].astype(F32)
        conv = jnp.concatenate([a[:8], b[:8]], 0)
        grad = jnp.concatenate([a[8:], b[8:]], 0)
        gq_ref[rows, :] = (c_ref[rows, :].astype(F32) * conv).astype(BF16)
        gk_ref[rows, :] = (v_ref[rows, :].astype(F32) * grad).astype(BF16)
        gv_ref[rows, :] = (k_ref[rows, :].astype(F32) * grad).astype(BF16)
        return 0

    lax.fori_loop(0, CTX // 2, gates, 0)
    for f in range(8):
        v = d_ref[f // 4, f % 4].astype(F32)
        for q in range(Q):
            wide[q, pl.ds(f, CTX, stride=8), :] = v[q * CTX:(q + 1) * CTX]
    for q in range(Q):
        gf_ref[:, q * R:(q + 1) * R] = wide[q].astype(BF16)


def per_device(queries, key_branch, value_branch, filters, cotangent):
    vmem = pl.BlockSpec(memory_space=pltpu.VMEM)
    tabs = [jnp.asarray(t) for t in tables()]
    dma = pltpu.SemaphoreType.DMA
    out, fil = pl.pallas_call(
        exchange_kernel,
        out_shape=(
            jax.ShapeDtypeStruct((CTX, 16, TOK), BF16),
            jax.ShapeDtypeStruct((2, 4, R, R), BF16),
        ),
        in_specs=[vmem] * 11,
        out_specs=(vmem, vmem),
        scratch_shapes=[
            pltpu.VMEM((CTX, 16, TOK), BF16),
            pltpu.VMEM((CTX, 16, TOK), BF16),
            pltpu.VMEM((CTX, 16, TOK), BF16),
            pltpu.VMEM((CTX, 16, TOK), BF16),
            pltpu.VMEM((Q, 256, R), F32),
            pltpu.VMEM((CTX, 16, R), BF16),
            pltpu.VMEM((2, CTX, 16, R), BF16),
            pltpu.VMEM((Q, CTX * 16, R), F32),
            pltpu.VMEM((2, CTX * 16, R), F32),
            pltpu.VMEM((16, R, 2 * R), F32),
            pltpu.VMEM((8, R, 2 * R), F32),
            pltpu.VMEM((8, R, R), F32),
            pltpu.VMEM((4, R, R), F32),
            pltpu.VMEM((4, R, R), BF16),
            pltpu.VMEM((4, R, R), BF16),
            pltpu.VMEM((R, R), F32),
            pltpu.VMEM((CTX, Q, R), F32),
            pltpu.VMEM((CTX, Q, R), F32),
            pltpu.VMEM((R, R), F32),
            pltpu.VMEM((2, 4, R, R), BF16),
            dma((32,)), dma((32,)), dma((32,)), dma((32,)), dma((32,)), dma((32,)),
            dma((32,)), dma((32,)), dma((4,)), dma((4,)), dma((4,)), dma((4,)), dma((3,)), dma((3,)),
        ],
        compiler_params=pltpu.CompilerParams(
            collective_id=0, has_side_effects=True, vmem_limit_bytes=40 * 2**20),
        name="exchange",
    )(queries, key_branch, value_branch, filters, cotangent, *tabs)
    block = jax.ShapeDtypeStruct((256, TOK), BF16)
    return pl.pallas_call(
        finish_kernel,
        out_shape=(block,) * 4,
        in_specs=[vmem] * 5,
        out_specs=(vmem,) * 4,
        scratch_shapes=[pltpu.VMEM((Q, 256, R), F32)],
        compiler_params=pltpu.CompilerParams(vmem_limit_bytes=32 * 2**20),
        name="finish",
    )(out, fil, cotangent, key_branch, value_branch)


def solution(mesh):
    placed = (P("tp", "ctx"), P("tp", "ctx"), P("tp", "ctx"), P(None, "ctx"), P("tp", "ctx"))
    return jax.shard_map(
        per_device,
        mesh=mesh,
        in_specs=placed,
        out_specs=(P("tp", "ctx"), P("tp", "ctx"), P("tp", "ctx"), P(None, "ctx")),
        check_vma=False,
    )
```

time: 330 us -> 80.4 us (0.24); the launches traced: 326 us -> 79.9 us
  matrix products: 131 us -> 0 us
  waiting for transfers between devices: 119 us -> 0 us
  Pallas kernels: 0 us -> 69.3 us
  starting transfers between devices: 50.8 us -> 0 us
  between operations: 14.8 us -> 0.66 us
  other arithmetic: 5.76 us -> 0 us
  local copies, waits for them, and re-layouts: 4.33 us -> 9.97 us
    dot_general x36 -> x0, matrix products: 131 us -> none  [product(): jnp.einsum(form, left.astype(jnp.bfloat16), right.astype(jnp.bfloat16), p...]
    psum x1 -> x0, waiting for transfers between devices: 78.5 us -> none  [conv_core(): summed = lax.psum(tap_terms.astype(jnp.bfloat16), 'tp').astype(jnp.float32)]
    pallas_call x0 -> x2, Pallas kernels: none -> 69.3 us  [the longest x1 68.1 us: per_device(): pl.pallas_call(exchange_kernel, out_shape=(jax.ShapeDtypeStruct((CTX, 16,...]
    all_to_all x6 -> x0, starting transfers between devices: 50.8 us -> none  [the longest x1 14.6 us: per_device(): lax.all_to_all(split_rows(grad_conv), 'ctx', split_axis=0, concat_axis=0,...]
    all_to_all x6 -> x0, waiting for transfers between devices: 40.9 us -> none  [the longest x1 11.1 us: per_device(): lax.all_to_all(split_rows(filters), 'ctx', split_axis=0, concat_axis=0, t...]
    unnamed x19 -> x22, local copies, waits for them, and re-layouts: 1.77 us -> 9.97 us
  transfers between devices with their start and end apart: 7 -> 0, of which waited for: 5 -> 0; matrix products, arithmetic and copies ran while one was open for 11% -> 0% of each run, Pallas kernels for 0% -> 0%
where the time goes in v1:
time: 80.4 us; the launch traced here: 79.9 us
  Pallas kernels  69.3 us (86%)
  local copies, waits for them, and re-layouts  9.97 us (12%)
    pallas_call x1, Pallas kernels, per_device(): pl.pallas_call(exchange_kernel, out_shape=(jax.ShapeDtypeStruct((CTX, 16,...  68.1 us
    unnamed x22, local copies, waits for them, and re-layouts  9.97 us

profile of v1, /device:TPU:1, one launch (start us, length us, event | category | flops | bytes accessed | tf_op | source)
XLA Modules:
  0.0 79.9 jit_solution(14425718502852304970)
XLA Ops:
  0.6 0.0 copy-start
  0.6 0.9 %copy-done = bf16[256,512]{1,0:T(8,128)(2,1)S(1)} copy-done((bf16[256,512]{1,0:T(8,128)(2,1)S(1)}, bf16[256,512]{1,0:T(8,128)(2,1)}, u32[]{:S(2)}) %copy-start) | copy-done | bytes 262168
  1.6 0.0 copy-start.1
  1.6 0.9 %copy-done.1 = bf16[256,512]{1,0:T(8,128)(2,1)S(1)} copy-done((bf16[256,512]{1,0:T(8,128)(2,1)S(1)}, bf16[256,512]{1,0:T(8,128)(2,1)}, u32[]{:S(2)}) %copy-start.1) | copy-done | bytes 262168
  2.5 0.0 copy-start.2
  2.5 0.9 %copy-done.2 = bf16[256,512]{1,0:T(8,128)(2,1)S(1)} copy-done((bf16[256,512]{1,0:T(8,128)(2,1)S(1)}, bf16[256,512]{1,0:T(8,128)(2,1)}, u32[]{:S(2)}) %copy-start.2) | copy-done | bytes 262168
  3.5 0.0 copy-start.3
  3.5 0.9 %copy-done.3 = bf16[256,512]{1,0:T(8,128)(2,1)S(1)} copy-done((bf16[256,512]{1,0:T(8,128)(2,1)S(1)}, bf16[256,512]{1,0:T(8,128)(2,1)}, u32[]{:S(2)}) %copy-start.3) | copy-done | bytes 262168
  4.4 0.0 copy-start.4
  4.4 0.9 %copy-done.4 = bf16[256,512]{1,0:T(8,128)(2,1)S(1)} copy-done((bf16[256,512]{1,0:T(8,128)(2,1)S(1)}, bf16[256,512]{1,0:T(8,128)(2,1)}, u32[]{:S(2)}) %copy-start.4) | copy-done | bytes 262168
  5.4 0.0 copy-start.5
  5.4 0.9 %copy-done.5 = bf16[256,256]{1,0:T(8,128)(2,1)S(1)} copy-done((bf16[256,256]{1,0:T(8,128)(2,1)S(1)}, bf16[256,256]{1,0:T(8,128)(2,1)}, u32[]{:S(2)}) %copy-start.5) | copy-done | bytes 131096
  6.3 0.0 copy-start.6
  6.3 0.9 %copy-done.6 = bf16[256,256]{1,0:T(8,128)(2,1)S(1)} copy-done((bf16[256,256]{1,0:T(8,128)(2,1)S(1)}, bf16[256,256]{1,0:T(8,128)(2,1)}, u32[]{:S(2)}) %copy-start.6) | copy-done | bytes 131096
  7.2 0.0 copy-start.7
  7.2 0.9 %copy-done.7 = f32[2,128,128]{2,1,0:T(8,128)S(1)} copy-done((f32[2,128,128]{2,1,0:T(8,128)S(1)}, f32[2,128,128]{2,1,0:T(8,128)}, u32[]{:S(2)}) %copy-start.7) | copy-done | bytes 131096
  8.1 0.0 copy-start.8
  8.1 0.8 %copy-done.8 = bf16[128,256]{1,0:T(8,128)(2,1)S(1)} copy-done((bf16[128,256]{1,0:T(8,128)(2,1)S(1)}, bf16[128,256]{1,0:T(8,128)(2,1)}, u32[]{:S(2)}) %copy-start.8) | copy-done | bytes 65560
  8.9 0.0 copy-start.9
  8.9 0.8 %copy-done.9 = bf16[128,256]{1,0:T(8,128)(2,1)S(1)} copy-done((bf16[128,256]{1,0:T(8,128)(2,1)S(1)}, bf16[128,256]{1,0:T(8,128)(2,1)}, u32[]{:S(2)}) %copy-start.9) | copy-done | bytes 65560
  9.8 0.0 copy-start.10
  9.8 0.8 %copy-done.10 = bf16[256,128]{1,0:T(8,128)(2,1)S(1)} copy-done((bf16[256,128]{1,0:T(8,128)(2,1)S(1)}, bf16[256,128]{1,0:T(8,128)(2,1)}, u32[]{:S(2)}) %copy-start.10) | copy-done | bytes 65560
  10.6 68.1 %exchange.1 = (bf16[32,16,512]{2,1,0:T(8,128)(2,1)S(1)}, bf16[2,4,128,128]{3,2,1,0:T(8,128)(2,1)S(1)}) custom-call(bf16[256,512]{1,0:T(8,128)(2,1)S(1)} %copy-done.3, bf16[256,512]{1,0:T(8,128)(2,1)S(1)} %copy-done, bf16[256,512]{1,0:T(8,128)(2,1)S(1)} %copy-done.1, bf16[256,512]{1,0:T(8,128)(2,1)S(1)} %copy-done.4, bf16[256,512]{1,0:T(8,128)(2,1)S(1)} %copy-done.2, ...), custom_call_target="tpu_custom_call" | custom-call | tf_op jit(solution)/shard_map/exchange/pallas_call | solution.py:280
  78.7 1.2 %finish.1 = (bf16[256,512]{1,0:T(8,128)(2,1)}, bf16[256,512]{1,0:T(8,128)(2,1)}, bf16[256,512]{1,0:T(8,128)(2,1)}, bf16[256,512]{1,0:T(8,128)(2,1)}) custom-call(bf16[32,16,512]{2,1,0:T(8,128)(2,1)S(1)} %get-tuple-element.6.o_ref, bf16[2,4,128,128]{3,2,1,0:T(8,128)(2,1)S(1)} %get-tuple-element.7.d_ref, bf16[256,512]{1,0:T(8,128)(2,1)S(1)} %copy-done.2, ...), custom_call_target="tpu_custom_call" | custom-call | tf_op jit(solution)/shard_map/finish/pallas_call | solution.py:317
Async XLA Ops:
  0.6 1.0 %copy-start = (bf16[256,512]{1,0:T(8,128)(2,1)S(1)}, bf16[256,512]{1,0:T(8,128)(2,1)}, u32[]{:S(2)}) copy-start(bf16[256,512]{1,0:T(8,128)(2,1)} %k_ref.3) | copy-start | bytes 786436
  1.6 0.9 %copy-start.1 = (bf16[256,512]{1,0:T(8,128)(2,1)S(1)}, bf16[256,512]{1,0:T(8,128)(2,1)}, u32[]{:S(2)}) copy-start(bf16[256,512]{1,0:T(8,128)(2,1)} %v_ref.3) | copy-start | bytes 786436
  2.5 0.9 %copy-start.2 = (bf16[256,512]{1,0:T(8,128)(2,1)S(1)}, bf16[256,512]{1,0:T(8,128)(2,1)}, u32[]{:S(2)}) copy-start(bf16[256,512]{1,0:T(8,128)(2,1)} %c_ref.3) | copy-start | bytes 786436
  3.5 0.9 %copy-start.3 = (bf16[256,512]{1,0:T(8,128)(2,1)S(1)}, bf16[256,512]{1,0:T(8,128)(2,1)}, u32[]{:S(2)}) copy-start(bf16[256,512]{1,0:T(8,128)(2,1)} %q_ref.1) | copy-start | bytes 786436
  4.4 0.9 %copy-start.4 = (bf16[256,512]{1,0:T(8,128)(2,1)S(1)}, bf16[256,512]{1,0:T(8,128)(2,1)}, u32[]{:S(2)}) copy-start(bf16[256,512]{1,0:T(8,128)(2,1)} %f_ref.1) | copy-start | bytes 786436
  5.4 0.9 %copy-start.5 = (bf16[256,256]{1,0:T(8,128)(2,1)S(1)}, bf16[256,256]{1,0:T(8,128)(2,1)}, u32[]{:S(2)}) copy-start(bf16[256,256]{1,0:T(8,128)(2,1)} %constant.15.clone.fi) | copy-start | bytes 393220
  6.3 0.9 %copy-start.6 = (bf16[256,256]{1,0:T(8,128)(2,1)S(1)}, bf16[256,256]{1,0:T(8,128)(2,1)}, u32[]{:S(2)}) copy-start(bf16[256,256]{1,0:T(8,128)(2,1)} %constant.14.clone.fw) | copy-start | bytes 393220
  7.2 0.9 %copy-start.7 = (f32[2,128,128]{2,1,0:T(8,128)S(1)}, f32[2,128,128]{2,1,0:T(8,128)}, u32[]{:S(2)}) copy-start(f32[2,128,128]{2,1,0:T(8,128)} %constant.13.clone.tw) | copy-start | bytes 393220
  8.1 0.8 %copy-start.8 = (bf16[128,256]{1,0:T(8,128)(2,1)S(1)}, bf16[128,256]{1,0:T(8,128)(2,1)}, u32[]{:S(2)}) copy-start(bf16[128,256]{1,0:T(8,128)(2,1)} %constant.17.clone.e1n) | copy-start | bytes 196612
  8.9 0.8 %copy-start.9 = (bf16[128,256]{1,0:T(8,128)(2,1)S(1)}, bf16[128,256]{1,0:T(8,128)(2,1)}, u32[]{:S(2)}) copy-start(bf16[128,256]{1,0:T(8,128)(2,1)} %constant.16.clone.e1q) | copy-start | bytes 196612
  9.8 0.8 %copy-start.10 = (bf16[256,128]{1,0:T(8,128)(2,1)S(1)}, bf16[256,128]{1,0:T(8,128)(2,1)}, u32[]{:S(2)}) copy-start(bf16[256,128]{1,0:T(8,128)(2,1)} %constant.12.clone.e1) | copy-start | bytes 196612

commit v2 on v0

v2 whole, which is shorter than its diff:
```python
import jax
import jax.numpy as jnp
import ml_dtypes
import numpy as np
from jax import lax
from jax.experimental import pallas as pl
from jax.experimental.pallas import tpu as pltpu
from jax.sharding import PartitionSpec as P

MESH = pl.DeviceIdType.MESH
F32 = jnp.float32
BF16 = jnp.bfloat16

SEQ = 16384
FILTERS = 256
CTX = 32
TP = 8
TOK = SEQ // CTX
R = 128
Q = TOK // R
SCALE = 2.0**-21


def tables():
    k = np.arange(R, dtype=np.float64)[:, None]
    n = np.arange(R, dtype=np.float64)[None, :]
    angle = 2 * np.pi * (k + 0.25) * n / R
    outer = np.concatenate([np.cos(angle), -np.sin(angle)], 0)
    order = np.arange(R).reshape(CTX, Q).T.reshape(-1)
    twist = 2 * np.pi * (k + 0.25) * n / SEQ
    inner = 2 * np.pi * ((k * n) % R) / R
    c, s = np.cos(inner), np.sin(inner)
    fwd = np.block([[c, -s], [s, c]])
    as_bf16 = lambda t: np.asarray(t, np.float32).astype(ml_dtypes.bfloat16)
    return (
        as_bf16(outer[:, order]),
        np.stack([np.cos(twist), np.sin(twist)]).astype(np.float32),
        as_bf16(fwd),
        as_bf16(fwd.T),
        as_bf16(outer.T[order]),
        as_bf16(outer.T),
    )


def dot(a, b):
    return jnp.dot(a, b, preferred_element_type=F32)


def exchange_kernel(
    q_hbm, k_hbm, v_hbm, f_hbm, c_hbm, e1_hbm, tw_hbm, fw_hbm, fi_hbm, e1q_hbm, e1n_hbm,
    out_ref, fil_ref,
    q_ref, k_ref, v_ref, f_ref, c_ref, e1, tw, fw, fi, e1q, e1n, s_l,
    snd, rcv, osnd, orcv, fsnd, frcv, csnd, crcv,
    wide, fwide, fflat, win, wout, acc,
    s_in, r_in, s_f, r_f, s_out, r_out, s_c, r_c, s_x, r_x, s_own,
):
    me = lax.axis_index("ctx")
    tp = lax.axis_index("tp")
    core = tp % 2
    zlo = tp // 2
    mx, mz, my = me % 4, (me // 4) % 2, me // 8
    mine = me * TP + tp
    xs = [(mx + i) % 4 for i in range(4)]
    ys = [((my + i) % 4) * 8 for i in range(4)]
    zs = [mz * 4, (1 - mz) * 4]
    cs = [ys[j // 4] + xs[j % 4] + zs[1] for j in range(16)]
    cs += [ys[j // 4] + xs[j % 4] + zs[0] for j in range(1, 16)]
    all_cs = cs + [me]
    ts = [(tp + d) % TP for d in range(TP)]
    back = [(tp + TP - d) % TP for d in range(TP)]
    chips = [((zlo + d) % 4) * 2 + core for d in range(4)]
    mate = zlo * 2 + 1 - core

    def remote(src, dst, ss, rs, c, t):
        return pltpu.make_async_remote_copy(
            src_ref=src, dst_ref=dst, send_sem=ss, recv_sem=rs, device_id=(c, t), device_id_type=MESH)

    def drain(ref, sem):
        pltpu.make_async_copy(ref, ref, sem).wait()

    loads = [
        pltpu.make_async_copy(src, dst, s_l.at[i])
        for i, (src, dst) in enumerate((
            (k_hbm, k_ref), (v_hbm, v_ref), (c_hbm, c_ref), (q_hbm, q_ref), (f_hbm, f_ref), (e1_hbm, e1),
            (tw_hbm, tw), (fw_hbm, fw), (fi_hbm, fi), (e1q_hbm, e1q), (e1n_hbm, e1n)))
    ]
    for load in loads:
        load.start()

    barrier = pltpu.get_barrier_semaphore()
    for d in range(TP):
        for c in cs if d == 0 else all_cs:
            pl.semaphore_signal(barrier, inc=1, device_id=(c, ts[d]), device_id_type=MESH)

    for load in loads[:4]:
        load.wait()
    for q in range(Q):
        lanes = slice(q * R, (q + 1) * R)
        wide[pl.ds(q, FILTERS, stride=8), :] = k_ref[:, lanes].astype(F32) * v_ref[:, lanes].astype(F32)
        wide[pl.ds(Q + q, FILTERS, stride=8), :] = c_ref[:, lanes].astype(F32) * q_ref[:, lanes].astype(F32)
    snd[...] = wide[...].reshape(FILTERS, 8, R).astype(BF16)
    pl.semaphore_wait(barrier, CTX * TP - 1)

    def send_in(d):
        for c in cs if d == 0 else all_cs:
            remote(snd.at[c * TP + ts[d]], rcv.at[tp, me], s_in.at[0], r_in.at[d], c, ts[d]).start()

    own_in = pltpu.make_async_copy(snd.at[mine], rcv.at[tp, me], r_in.at[0])
    own_in.start()
    send_in(0)

    loads[4].wait()
    for q in range(Q):
        fwide[q] = f_ref[:, q * R:(q + 1) * R].astype(F32)
    for q in range(Q):
        fflat[pl.ds(q, CTX, stride=Q), :] = fwide[q, pl.ds(tp, CTX, stride=TP), :]
    for c in range(CTX):
        fsnd[c] = fflat[c * Q:(c + 1) * Q, :].astype(BF16)
    own_f = pltpu.make_async_copy(fsnd.at[me], frcv.at[me], r_f.at[0])
    own_f.start()
    for c in cs:
        remote(fsnd.at[c], frcv.at[me], s_f.at[0], r_f.at[0], c, tp).start()
    for d in range(1, TP):
        send_in(d)

    def forward(x):
        y = dot(e1[...], x)
        yr, yi = y[:R], y[R:]
        tc, ts_ = tw[0], tw[1]
        left = jnp.concatenate([(yr * tc + yi * ts_).astype(BF16), (yi * tc - yr * ts_).astype(BF16)], 1)
        z = dot(left, fw[...])
        return z[:, :R], z[:, R:]

    def inverse(pr, pi, out):
        u = dot(jnp.concatenate([pr.astype(BF16), pi.astype(BF16)], 1), fi[...])
        ur, ui = u[:, :R], u[:, R:]
        tc, ts_ = tw[0], tw[1]
        v = jnp.concatenate([(ur * tc - ui * ts_).astype(BF16), (ui * tc + ur * ts_).astype(BF16)], 0)
        return dot(out[...], v) * SCALE

    for load in loads[5:]:
        load.wait()
    hr = hi = None
    for d in range(TP):
        drain(rcv.at[back[d]], r_in.at[d])
        win[d] = rcv[back[d]].astype(F32).reshape(CTX * 8, R)
        x = jnp.concatenate([win[d, pl.ds(q, CTX, stride=8), :] for q in range(Q)], 0)
        gr, gi = forward(x.astype(BF16))
        x = jnp.concatenate([win[d, pl.ds(Q + q, CTX, stride=8), :] for q in range(Q)], 0)
        dr, di = forward(x.astype(BF16))
        if d == 0:
            acc[0] = gr * dr + gi * di
            acc[1] = gr * di - gi * dr
            drain(frcv, r_f.at[0])
            for c in range(CTX):
                fflat[c * Q:(c + 1) * Q, :] = frcv[c].astype(F32)
            x = jnp.concatenate([fflat[pl.ds(q, CTX, stride=Q), :] for q in range(Q)], 0)
            hr, hi = forward(x.astype(BF16))
        else:
            acc[0] += gr * dr + gi * di
            acc[1] += gr * di - gi * dr
        if d == TP - 1:
            total = inverse(acc[0], acc[1], e1n)
            for c in range(CTX):
                csnd[c] = total[c * Q:(c + 1) * Q].astype(BF16)
            pltpu.make_async_copy(csnd.at[me], crcv.at[core, me * 4 + zlo], r_c.at[0]).start()
            for z in range(4):
                for c in cs if z == 0 else all_cs:
                    remote(csnd.at[c], crcv.at[core, me * 4 + zlo], s_c.at[0], r_c.at[0], c, chips[z]).start()
        conv = inverse(gr * hr - gi * hi, gr * hi + gi * hr, e1q)
        grad = inverse(hr * dr + hi * di, hr * di - hi * dr, e1q)
        for q in range(Q):
            wout[d, pl.ds(q, CTX, stride=8), :] = conv[q * CTX:(q + 1) * CTX]
            wout[d, pl.ds(Q + q, CTX, stride=8), :] = grad[q * CTX:(q + 1) * CTX]
        osnd[d] = wout[d].reshape(CTX, 8, R).astype(BF16)
        if d == 0:
            pltpu.make_async_copy(osnd.at[0, me], orcv.at[mine], r_out.at[0]).start()
        for c in cs if d == 0 else all_cs:
            remote(osnd.at[d, c], orcv.at[mine], s_out.at[0], r_out.at[0], c, back[d]).start()

    drain(crcv.at[core], r_c.at[0])
    swap = remote(crcv.at[core], crcv.at[core], s_x.at[0], r_x.at[0], me, mate)
    swap.start()
    drain(orcv, r_out.at[0])
    out_ref[...] = orcv[...]
    swap.wait()
    fil_ref[...] = crcv[...]

    drain(snd.at[pl.ds(0, CTX * TP - 1)], s_in.at[0])
    drain(snd.at[pl.ds(0, CTX * TP - 1)], s_out.at[0])
    drain(fsnd.at[pl.ds(0, CTX - 1)], s_f.at[0])
    drain(crcv.at[0, pl.ds(0, CTX * 4 - 1)], s_c.at[0])


def finish_kernel(o_ref, d_ref, c_ref, k_ref, v_ref, gq_ref, gk_ref, gv_ref, gf_ref, wide, fflat, fwide):
    wide[...] = o_ref[...].astype(F32).reshape(FILTERS * 8, R)
    for q in range(Q):
        lanes = slice(q * R, (q + 1) * R)
        conv = wide[pl.ds(q, FILTERS, stride=8), :]
        grad = wide[pl.ds(Q + q, FILTERS, stride=8), :]
        gq_ref[:, lanes] = (c_ref[:, lanes].astype(F32) * conv).astype(BF16)
        gk_ref[:, lanes] = (v_ref[:, lanes].astype(F32) * grad).astype(BF16)
        gv_ref[:, lanes] = (k_ref[:, lanes].astype(F32) * grad).astype(BF16)
    for k in range(2):
        for i in range(CTX * 4):
            fflat[k, i * Q:(i + 1) * Q, :] = d_ref[k, i].astype(F32)
    for q in range(Q):
        for k in range(2):
            fwide[pl.ds(k, CTX * 4, stride=2), :] = fflat[k, pl.ds(q, CTX * 4, stride=Q), :]
        gf_ref[:, q * R:(q + 1) * R] = fwide[...].astype(BF16)


def per_device(queries, key_branch, value_branch, filters, cotangent):
    vmem = pl.BlockSpec(memory_space=pltpu.VMEM)
    tabs = [jnp.asarray(t) for t in tables()]
    dma = pltpu.SemaphoreType.DMA
    out, fil = pl.pallas_call(
        exchange_kernel,
        out_shape=(
            jax.ShapeDtypeStruct((FILTERS, 8, R), BF16),
            jax.ShapeDtypeStruct((2, CTX * 4, Q, R), BF16),
        ),
        in_specs=[pl.BlockSpec(memory_space=pltpu.HBM)] * 11,
        out_specs=(vmem, vmem),
        scratch_shapes=[pltpu.VMEM((256, TOK), BF16)] * 5
        + [pltpu.VMEM(t.shape, t.dtype) for t in tabs]
        + [
            dma((11,)),
            pltpu.VMEM((FILTERS, 8, R), BF16),
            pltpu.VMEM((TP, CTX, 8, R), BF16),
            pltpu.VMEM((TP, CTX, 8, R), BF16),
            pltpu.VMEM((FILTERS, 8, R), BF16),
            pltpu.VMEM((CTX, Q, R), BF16),
            pltpu.VMEM((CTX, Q, R), BF16),
            pltpu.VMEM((CTX, Q, R), BF16),
            pltpu.VMEM((2, CTX * 4, Q, R), BF16),
            pltpu.VMEM((FILTERS * 8, R), F32),
            pltpu.VMEM((Q, FILTERS, R), F32),
            pltpu.VMEM((CTX * Q, R), F32),
            pltpu.VMEM((TP, CTX * 8, R), F32),
            pltpu.VMEM((TP, CTX * 8, R), F32),
            pltpu.VMEM((2, R, R), F32),
            dma((1,)), dma((TP,)), dma((1,)), dma((1,)), dma((1,)), dma((1,)),
            dma((1,)), dma((1,)), dma((1,)), dma((1,)), dma((1,)),
        ],
        compiler_params=pltpu.CompilerParams(
            collective_id=0, has_side_effects=True, vmem_limit_bytes=40 * 2**20),
        name="exchange",
    )(*(pltpu.with_memory_space_constraint(a, pltpu.HBM)
        for a in (queries, key_branch, value_branch, filters, cotangent, *tabs)))
    block = jax.ShapeDtypeStruct((256, TOK), BF16)
    return pl.pallas_call(
        finish_kernel,
        out_shape=(block,) * 4,
        in_specs=[vmem] * 5,
        out_specs=(vmem,) * 4,
        scratch_shapes=[
            pltpu.VMEM((FILTERS * 8, R), F32),
            pltpu.VMEM((2, CTX * 4 * Q, R), F32),
            pltpu.VMEM((FILTERS, R), F32),
        ],
        compiler_params=pltpu.CompilerParams(vmem_limit_bytes=32 * 2**20),
        name="finish",
    )(out, fil, cotangent, key_branch, value_branch)


def solution(mesh):
    placed = (P("tp", "ctx"), P("tp", "ctx"), P("tp", "ctx"), P(None, "ctx"), P("tp", "ctx"))
    return jax.shard_map(
        per_device,
        mesh=mesh,
        in_specs=placed,
        out_specs=(P("tp", "ctx"), P("tp", "ctx"), P("tp", "ctx"), P(None, "ctx")),
        check_vma=False,
    )
```

time: 330 us -> 47.6 us (0.14); the launches traced: 326 us -> 47.5 us
  matrix products: 131 us -> 0 us
  waiting for transfers between devices: 119 us -> 0 us
  starting transfers between devices: 50.8 us -> 0 us
  Pallas kernels: 0 us -> 46.8 us
  between operations: 14.8 us -> 0.69 us
  other arithmetic: 5.76 us -> 0 us
  local copies, waits for them, and re-layouts: 4.33 us -> 0.01 us
    dot_general x36 -> x0, matrix products: 131 us -> none  [product(): jnp.einsum(form, left.astype(jnp.bfloat16), right.astype(jnp.bfloat16), p...]
    psum x1 -> x0, waiting for transfers between devices: 78.5 us -> none  [conv_core(): summed = lax.psum(tap_terms.astype(jnp.bfloat16), 'tp').astype(jnp.float32)]
    all_to_all x6 -> x0, starting transfers between devices: 50.8 us -> none  [the longest x1 14.6 us: per_device(): lax.all_to_all(split_rows(grad_conv), 'ctx', split_axis=0, concat_axis=0,...]
    pallas_call x0 -> x2, Pallas kernels: none -> 46.8 us  [the longest x1 45.5 us: per_device(): pl.pallas_call(exchange_kernel, out_shape=(jax.ShapeDtypeStruct((FILTERS,...]
    all_to_all x6 -> x0, waiting for transfers between devices: 40.9 us -> none  [the longest x1 11.1 us: per_device(): lax.all_to_all(split_rows(filters), 'ctx', split_axis=0, concat_axis=0, t...]
  transfers between devices with their start and end apart: 7 -> 0, of which waited for: 5 -> 0; matrix products, arithmetic and copies ran while one was open for 11% -> 0% of each run, Pallas kernels for 0% -> 0%
where the time goes in v2:
time: 47.6 us; the launch traced here: 47.5 us
  Pallas kernels  46.8 us (98%)
  between operations  0.69 us (1%)
    pallas_call x1, Pallas kernels, per_device(): pl.pallas_call(exchange_kernel, out_shape=(jax.ShapeDtypeStruct((FILTERS,...  45.5 us
    pallas_call x1, Pallas kernels, per_device(): pl.pallas_call(finish_kernel, out_shape=(block,) * 4, in_specs=[vmem] * 5...  1.35 us

profile of v2, /device:TPU:1, one launch (start us, length us, event | category | flops | bytes accessed | tf_op | source)
XLA Modules:
  0.0 47.5 jit_solution(3771292171509331468)
XLA Ops:
  0.6 0.0 copy-start.2
  0.6 0.0 copy-start.1
  0.7 0.0 copy-start
  0.7 45.5 %exchange.1 = (bf16[256,8,128]{2,1,0:T(8,128)(2,1)S(1)}, bf16[2,128,4,128]{3,2,1,0:T(4,128)(2,1)S(1)}) custom-call(bf16[256,512]{1,0:T(8,128)(2,1)} %q_hbm.1, bf16[256,512]{1,0:T(8,128)(2,1)} %k_ref.1, bf16[256,512]{1,0:T(8,128)(2,1)} %v_ref.1, bf16[256,512]{1,0:T(8,128)(2,1)} %f_hbm.1, bf16[256,512]{1,0:T(8,128)(2,1)} %c_ref.1, ...), custom_call_target="tpu_custom_call" | custom-call | tf_op jit(solution)/shard_map/exchange/pallas_call | solution.py:217
  46.2 0.0 copy-done.2
  46.2 0.0 copy-done.1
  46.2 0.0 copy-done
  46.2 1.3 %finish.1 = (bf16[256,512]{1,0:T(8,128)(2,1)}, bf16[256,512]{1,0:T(8,128)(2,1)}, bf16[256,512]{1,0:T(8,128)(2,1)}, bf16[256,512]{1,0:T(8,128)(2,1)}) custom-call(bf16[256,8,128]{2,1,0:T(8,128)(2,1)S(1)} %get-tuple-element.6.o_ref, bf16[2,128,4,128]{3,2,1,0:T(4,128)(2,1)S(1)} %get-tuple-element.7.d_ref, bf16[256,512]{1,0:T(8,128)(2,1)S(1)} %copy-done.2, ...), custom_call_target="tpu_custom_call" | custom-call | tf_op jit(solution)/shard_map/finish/pallas_call | solution.py:252
Async XLA Ops:
  0.6 45.5 %copy-start.2 = (bf16[256,512]{1,0:T(8,128)(2,1)S(1)}, bf16[256,512]{1,0:T(8,128)(2,1)}, u32[]{:S(2)}) copy-start(bf16[256,512]{1,0:T(8,128)(2,1)} %c_ref.1) | copy-start | bytes 786436
  0.6 45.5 %copy-start.1 = (bf16[256,512]{1,0:T(8,128)(2,1)S(1)}, bf16[256,512]{1,0:T(8,128)(2,1)}, u32[]{:S(2)}) copy-start(bf16[256,512]{1,0:T(8,128)(2,1)} %v_ref.1) | copy-start | bytes 786436
  0.7 45.5 %copy-start = (bf16[256,512]{1,0:T(8,128)(2,1)S(1)}, bf16[256,512]{1,0:T(8,128)(2,1)}, u32[]{:S(2)}) copy-start(bf16[256,512]{1,0:T(8,128)(2,1)} %k_ref.1) | copy-start | bytes 786436

commit v3 on v2

v3 whole, which is shorter than its diff:
```python
import jax
import jax.numpy as jnp
import ml_dtypes
import numpy as np
from jax import lax
from jax.experimental import pallas as pl
from jax.experimental.pallas import tpu as pltpu
from jax.sharding import PartitionSpec as P

MESH = pl.DeviceIdType.MESH
F32 = jnp.float32
BF16 = jnp.bfloat16

SEQ = 16384
FILTERS = 256
CTX = 32
TP = 8
TOK = SEQ // CTX
R = 128
Q = TOK // R
SCALE = 2.0**-21


def tables():
    k = np.arange(R, dtype=np.float64)[:, None]
    n = np.arange(R, dtype=np.float64)[None, :]
    angle = 2 * np.pi * (k + 0.25) * n / R
    outer = np.concatenate([np.cos(angle), -np.sin(angle)], 0)
    pair = np.zeros((2, 2 * R, CTX, 2, Q))
    pair[0, :, :, 0] = pair[1, :, :, 1] = outer.reshape(2 * R, CTX, Q)
    pair = pair.reshape(4 * R, 2 * R)
    twist = 2 * np.pi * (k + 0.25) * n / SEQ
    inner = 2 * np.pi * ((k * n) % R) / R
    c, s = np.cos(inner), np.sin(inner)
    fwd = np.block([[c, -s], [s, c]])
    as_bf16 = lambda t: np.asarray(t, np.float32).astype(ml_dtypes.bfloat16)
    return (
        as_bf16(pair),
        np.stack([np.cos(twist), np.sin(twist)]).astype(np.float32),
        as_bf16(fwd),
        as_bf16(fwd.T),
        as_bf16(pair.T),
        as_bf16(outer),
        as_bf16(outer.T),
    )


def dot(a, b):
    return jnp.dot(a, b, preferred_element_type=F32)


def exchange_kernel(
    q_hbm, k_hbm, v_hbm, f_hbm, c_hbm, e2_hbm, tw_hbm, fw_hbm, fi_hbm, e2t_hbm, e1_hbm, e1t_hbm,
    out_ref, fil_ref, k_ref, v_ref, c_ref,
    q_ref, f_ref, e2, tw, fw, fi, e2t, e1, e1t, s_l,
    snd, rcv, osnd, fsnd, frcv, csnd,
    wide, fwide, fflat, acc, spec,
    s_in, r_in, s_f, r_f, s_out, r_out, s_c, r_c, s_x, r_x, known,
):
    me = lax.axis_index("ctx")
    tp = lax.axis_index("tp")
    core = tp % 2
    zlo = tp // 2
    mx, mz, my = me % 4, (me // 4) % 2, me // 8
    mine = me * TP + tp
    xs = [(mx + i) % 4 for i in range(4)]
    ys = [((my + i) % 4) * 8 for i in range(4)]
    zs = [mz * 4, (1 - mz) * 4]
    xys = [ys[j // 4] + xs[j % 4] for j in range(16)]
    near = [xy + zs[0] for xy in xys]
    far = [xy + zs[1] for xy in xys]
    cs = far + near[1:]
    all_cs = cs + [me]

    def beside(dz, dk):
        return ((zlo + dz) % 4) * 2 + (core + dk) % 2

    sets = (((0, 0), (0, 1)), ((1, 0), (3, 0)), ((1, 1), (3, 1)), ((2, 0), (2, 1)))
    chips = [beside(dz, 0) for dz in (0, 1, 3, 2)]
    mate = beside(0, 1)

    def remote(src, dst, ss, rs, c, t):
        return pltpu.make_async_remote_copy(
            src_ref=src, dst_ref=dst, send_sem=ss, recv_sem=rs, device_id=(c, t), device_id_type=MESH)

    def drain(ref, sem):
        pltpu.make_async_copy(ref, ref, sem).wait()

    loads = [
        pltpu.make_async_copy(src, dst, s_l.at[i])
        for i, (src, dst) in enumerate((
            (k_hbm, k_ref), (v_hbm, v_ref), (c_hbm, c_ref), (q_hbm, q_ref), (f_hbm, f_ref), (e2_hbm, e2),
            (tw_hbm, tw), (fw_hbm, fw), (fi_hbm, fi), (e2t_hbm, e2t), (e1_hbm, e1), (e1t_hbm, e1t)))
    ]
    for load in loads[:4]:
        load.start()

    barrier = pltpu.get_barrier_semaphore()
    for c in cs:
        for t in (tp, mate):
            pl.semaphore_signal(barrier, inc=1, device_id=(c, t), device_id_type=MESH)
    for t in (mate, *chips[1:]):
        pl.semaphore_signal(barrier, inc=1, device_id=(me, t), device_id_type=MESH)
    for load in loads[4:]:
        load.start()

    for load in loads[:4]:
        load.wait()
    for q in range(Q):
        lanes = slice(q * R, (q + 1) * R)
        wide[pl.ds(q, FILTERS, stride=8), :] = k_ref[:, lanes].astype(F32) * v_ref[:, lanes].astype(F32)
        wide[pl.ds(Q + q, FILTERS, stride=8), :] = c_ref[:, lanes].astype(F32) * q_ref[:, lanes].astype(F32)
    snd[...] = wide[...].reshape(FILTERS, 8, R).astype(BF16)
    pl.semaphore_wait(barrier, 2 * CTX - 1 + 3)
    for t in chips[1:]:
        pl.semaphore_signal(known, inc=1, device_id=(me, t), device_id_type=MESH)

    def send_in(n):
        for c in all_cs:
            for i, (dz, dk) in enumerate(sets[n]):
                if c is not me or dz or dk:
                    t = beside(dz, dk)
                    remote(snd.at[c * TP + t], rcv.at[tp, me], s_in.at[0], r_in.at[n, i], c, t).start()

    pltpu.make_async_copy(snd.at[mine], rcv.at[tp, me], r_in.at[0, 0]).start()
    send_in(0)

    loads[4].wait()
    for q in range(Q):
        fwide[q] = f_ref[:, q * R:(q + 1) * R].astype(F32)
    for q in range(Q):
        fflat[pl.ds(q, CTX, stride=Q), :] = fwide[q, pl.ds(tp, CTX, stride=TP), :]
    fsnd[...] = fflat[...].astype(BF16).reshape(CTX, Q, R)
    own_f = pltpu.make_async_copy(fsnd.at[me], frcv.at[me], r_f.at[0])
    own_f.start()
    for c in cs:
        remote(fsnd.at[c], frcv.at[me], s_f.at[0], r_f.at[0], c, tp).start()
    pl.semaphore_wait(known, 3)
    for n in range(1, 4):
        send_in(n)

    def twist(y):
        yr, yi = y[:R], y[R:]
        tc, ts_ = tw[0], tw[1]
        return jnp.concatenate([(yr * tc + yi * ts_).astype(BF16), (yi * tc - yr * ts_).astype(BF16)], 1)

    def untwist(u):
        ur, ui = u[:, :R], u[:, R:]
        tc, ts_ = tw[0], tw[1]
        return jnp.concatenate([(ur * tc - ui * ts_).astype(BF16), (ui * tc + ur * ts_).astype(BF16)], 0)

    def pack(pr, pi):
        return jnp.concatenate([pr.astype(BF16), pi.astype(BF16)], 1)

    for load in loads[5:]:
        load.wait()
    def sources(n):
        return [beside(4 - dz, dk) for dz, dk in sets[n]]

    def analyse(n):
        left = []
        for i, t in enumerate(sources(n)):
            drain(rcv.at[t], r_in.at[n, i])
        for i, t in enumerate(sources(n)):
            y = dot(e2[...], rcv[t].reshape(CTX * 8, R))
            left += [twist(y[:2 * R]), twist(y[2 * R:])]
        z = dot(jnp.concatenate(left, 0), fw[...])
        for i in range(2):
            g, d = z[2 * i * R:(2 * i + 1) * R], z[(2 * i + 1) * R:(2 * i + 2) * R]
            gr, gi, dr, di = g[:, :R], g[:, R:], d[:, :R], d[:, R:]
            sr, si = gr * dr + gi * di, gr * di - gi * dr
            if n == 0 and i == 0:
                acc[0], acc[1] = sr, si
            else:
                acc[0] += sr
                acc[1] += si
            spec[2 * n + i, 0], spec[2 * n + i, 1], spec[2 * n + i, 2], spec[2 * n + i, 3] = gr, gi, dr, di

    def results(n):
        hr, hi = acc[2], acc[3]
        parts = []
        for i in range(2):
            gr, gi, dr, di = (spec[2 * n + i, j] for j in range(4))
            parts += [pack(gr * hr - gi * hi, gr * hi + gi * hr), pack(hr * dr + hi * di, hr * di - hi * dr)]
        u = dot(jnp.concatenate(parts, 0), fi[...])
        for i in range(2):
            v = [untwist(u[j * R:(j + 1) * R]) for j in (2 * i, 2 * i + 1)]
            y = dot(e2t[...], jnp.concatenate(v, 0)) * SCALE
            osnd[2 * n + i] = y.astype(BF16).reshape(CTX, 8, R)
        if n == 0:
            pltpu.make_async_copy(osnd.at[0, me], out_ref.at[mine], r_out.at[0]).start()
        for c in all_cs:
            for i, t in enumerate(sources(n)):
                if c is not me or n or i:
                    remote(osnd.at[2 * n + i, c], out_ref.at[mine], s_out.at[0], r_out.at[0], c, t).start()

    def filter_gradient():
        u = dot(pack(acc[0], acc[1]), fi[...])
        total = dot(e1t[...], untwist(u)) * SCALE
        csnd[...] = total.astype(BF16).reshape(CTX, Q, R)
        place = fil_ref.at[core, me * 4 + zlo]
        pltpu.make_async_copy(csnd.at[me], place, r_c.at[0]).start()
        for c in all_cs:
            for i, t in enumerate(chips):
                if c is not me or i:
                    remote(csnd.at[c], place, s_c.at[0], r_c.at[0], c, t).start()

    analyse(0)
    drain(frcv, r_f.at[0])
    h = dot(twist(dot(e1[...], frcv[...].reshape(CTX * Q, R))), fw[...])
    acc[2], acc[3] = h[:, :R], h[:, R:]
    results(0)
    analyse(1)
    results(1)
    analyse(2)
    results(2)
    analyse(3)
    filter_gradient()
    results(3)

    drain(fil_ref.at[core], r_c.at[0])
    swap = remote(fil_ref.at[core], fil_ref.at[core], s_x.at[0], r_x.at[0], me, mate)
    swap.start()
    drain(out_ref, r_out.at[0])
    swap.wait()

    drain(snd.at[pl.ds(0, CTX * TP - 1)], s_in.at[0])
    drain(snd.at[pl.ds(0, CTX * TP - 1)], s_out.at[0])
    drain(fsnd.at[pl.ds(0, CTX - 1)], s_f.at[0])
    drain(fil_ref.at[0, pl.ds(0, CTX * 4 - 1)], s_c.at[0])


def finish_kernel(o_ref, d_ref, c_ref, k_ref, v_ref, gq_ref, gk_ref, gv_ref, gf_ref, wide, fflat, fwide):
    wide[...] = o_ref[...].astype(F32).reshape(FILTERS * 8, R)
    for q in range(Q):
        lanes = slice(q * R, (q + 1) * R)
        conv = wide[pl.ds(q, FILTERS, stride=8), :]
        grad = wide[pl.ds(Q + q, FILTERS, stride=8), :]
        gq_ref[:, lanes] = (c_ref[:, lanes].astype(F32) * conv).astype(BF16)
        gk_ref[:, lanes] = (v_ref[:, lanes].astype(F32) * grad).astype(BF16)
        gv_ref[:, lanes] = (k_ref[:, lanes].astype(F32) * grad).astype(BF16)
    fflat[...] = d_ref[...].astype(F32).reshape(2, CTX * 4 * Q, R)
    for q in range(Q):
        for k in range(2):
            fwide[pl.ds(k, CTX * 4, stride=2), :] = fflat[k, pl.ds(q, CTX * 4, stride=Q), :]
        gf_ref[:, q * R:(q + 1) * R] = fwide[...].astype(BF16)


def per_device(queries, key_branch, value_branch, filters, cotangent):
    vmem = pl.BlockSpec(memory_space=pltpu.VMEM)
    tabs = [jnp.asarray(t) for t in tables()]
    dma = pltpu.SemaphoreType.DMA
    block = jax.ShapeDtypeStruct((256, TOK), BF16)
    out, fil, key, value, cot = pl.pallas_call(
        exchange_kernel,
        out_shape=(
            jax.ShapeDtypeStruct((FILTERS, 8, R), BF16),
            jax.ShapeDtypeStruct((2, CTX * 4, Q, R), BF16),
            block, block, block,
        ),
        in_specs=[pl.BlockSpec(memory_space=pltpu.HBM)] * 12,
        out_specs=(vmem,) * 5,
        scratch_shapes=[pltpu.VMEM((256, TOK), BF16)] * 2
        + [pltpu.VMEM(t.shape, t.dtype) for t in tabs]
        + [
            dma((12,)),
            pltpu.VMEM((FILTERS, 8, R), BF16),
            pltpu.VMEM((TP, CTX, 8, R), BF16),
            pltpu.VMEM((TP, CTX, 8, R), BF16),
            pltpu.VMEM((CTX, Q, R), BF16),
            pltpu.VMEM((CTX, Q, R), BF16),
            pltpu.VMEM((CTX, Q, R), BF16),
            pltpu.VMEM((FILTERS * 8, R), F32),
            pltpu.VMEM((Q, FILTERS, R), F32),
            pltpu.VMEM((CTX * Q, R), F32),
            pltpu.VMEM((4, R, R), F32),
            pltpu.VMEM((TP, 4, R, R), F32),
            dma((1,)), dma((4, 2)), dma((1,)), dma((1,)), dma((1,)), dma((1,)),
            dma((1,)), dma((1,)), dma((1,)), dma((1,)), pltpu.SemaphoreType.REGULAR,
        ],
        compiler_params=pltpu.CompilerParams(
            collective_id=0, has_side_effects=True, vmem_limit_bytes=40 * 2**20),
        name="exchange",
    )(*(pltpu.with_memory_space_constraint(a, pltpu.HBM)
        for a in (queries, key_branch, value_branch, filters, cotangent, *tabs)))
    return pl.pallas_call(
        finish_kernel,
        out_shape=(block,) * 4,
        in_specs=[vmem] * 5,
        out_specs=(vmem,) * 4,
        scratch_shapes=[
            pltpu.VMEM((FILTERS * 8, R), F32),
            pltpu.VMEM((2, CTX * 4 * Q, R), F32),
            pltpu.VMEM((FILTERS, R), F32),
        ],
        compiler_params=pltpu.CompilerParams(vmem_limit_bytes=32 * 2**20),
        name="finish",
    )(out, fil, cot, key, value)


def solution(mesh):
    placed = (P("tp", "ctx"), P("tp", "ctx"), P("tp", "ctx"), P(None, "ctx"), P("tp", "ctx"))
    return jax.shard_map(
        per_device,
        mesh=mesh,
        in_specs=placed,
        out_specs=(P("tp", "ctx"), P("tp", "ctx"), P("tp", "ctx"), P(None, "ctx")),
        check_vma=False,
    )
```

time: 47.6 us -> 46.7 us (0.981)
  Pallas kernels: 46.8 us -> 45.9 us
    pallas_call x1, Pallas kernels: 45.5 us -> 44.5 us  [per_device(): pl.pallas_call(exchange_kernel, out_shape=(jax.ShapeDtypeStruct((FILTERS,...]
where the time goes in v3:
time: 46.7 us; the launch traced here: 46.6 us
  Pallas kernels  45.9 us (98%)
  between operations  0.64 us (1%)
    pallas_call x1, Pallas kernels, per_device(): pl.pallas_call(exchange_kernel, out_shape=(jax.ShapeDtypeStruct((FILTERS,...  44.5 us
    pallas_call x1, Pallas kernels, per_device(): pl.pallas_call(finish_kernel, out_shape=(block,) * 4, in_specs=[vmem] * 5...  1.38 us

profile of v3, /device:TPU:1, one launch (start us, length us, event | category | flops | bytes accessed | tf_op | source)
XLA Modules:
  0.0 46.6 jit_solution(9321544413673753114)
XLA Ops:
  0.6 44.5 %exchange.1 = (bf16[256,8,128]{2,1,0:T(8,128)(2,1)S(1)}, bf16[2,128,4,128]{3,2,1,0:T(4,128)(2,1)S(1)}, bf16[256,512]{1,0:T(8,128)(2,1)S(1)}, bf16[256,512]{1,0:T(8,128)(2,1)S(1)}, bf16[256,512]{1,0:T(8,128)(2,1)S(1)}) custom-call(bf16[256,512]{1,0:T(8,128)(2,1)} %q_hbm.1, bf16[256,512]{1,0:T(8,128)(2,1)} %k_hbm.1, bf16[256,512]{1,0:T(8,128)(2,1)} %v_hbm.1, ...), custom_call_target="tpu_custom_call" | custom-call | tf_op jit(solution)/shard_map/exchange/pallas_call | solution.py:254
  45.2 1.4 %finish.1 = (bf16[256,512]{1,0:T(8,128)(2,1)}, bf16[256,512]{1,0:T(8,128)(2,1)}, bf16[256,512]{1,0:T(8,128)(2,1)}, bf16[256,512]{1,0:T(8,128)(2,1)}) custom-call(bf16[256,8,128]{2,1,0:T(8,128)(2,1)S(1)} %get-tuple-element.9.o_ref, bf16[2,128,4,128]{3,2,1,0:T(4,128)(2,1)S(1)} %get-tuple-element.10.d_ref, bf16[256,512]{1,0:T(8,128)(2,1)S(1)} %get-tuple-element.11.c_ref, ...), custom_call_target="tpu_custom_call" | custom-call | tf_op jit(solution)/shard_map/finish/pallas_call | solution.py:286

commit v4 on v3

--- a/solution.py
+++ b/solution.py
@@ -75,7 +75,7 @@
     def beside(dz, dk):
         return ((zlo + dz) % 4) * 2 + (core + dk) % 2
 
-    sets = (((0, 0), (0, 1)), ((1, 0), (3, 0)), ((1, 1), (3, 1)), ((2, 0), (2, 1)))
+    sets = (((0, 0), (0, 1)), ((2, 0), (2, 1)), ((1, 0), (3, 0)), ((1, 1), (3, 1)))
     chips = [beside(dz, 0) for dz in (0, 1, 3, 2)]
     mate = beside(0, 1)
 

time: 46.7 us -> 45.5 us (0.974)
  Pallas kernels: 45.9 us -> 44.8 us
    pallas_call x1, Pallas kernels: 44.5 us -> 43.4 us  [per_device(): pl.pallas_call(exchange_kernel, out_shape=(jax.ShapeDtypeStruct((FILTERS,...]
where the time goes in v4:
time: 45.5 us; the launch traced here: 45.4 us
  Pallas kernels  44.8 us (98%)
  between operations  0.64 us (1%)
    pallas_call x1, Pallas kernels, per_device(): pl.pallas_call(exchange_kernel, out_shape=(jax.ShapeDtypeStruct((FILTERS,...  43.4 us
    pallas_call x1, Pallas kernels, per_device(): pl.pallas_call(finish_kernel, out_shape=(block,) * 4, in_specs=[vmem] * 5...  1.38 us

profile of v4, /device:TPU:1, one launch (start us, length us, event | category | flops | bytes accessed | tf_op | source)
XLA Modules:
  0.0 45.4 jit_solution(3277093719593107701)
XLA Ops:
  0.6 43.4 %exchange.1 = (bf16[256,8,128]{2,1,0:T(8,128)(2,1)S(1)}, bf16[2,128,4,128]{3,2,1,0:T(4,128)(2,1)S(1)}, bf16[256,512]{1,0:T(8,128)(2,1)S(1)}, bf16[256,512]{1,0:T(8,128)(2,1)S(1)}, bf16[256,512]{1,0:T(8,128)(2,1)S(1)}) custom-call(bf16[256,512]{1,0:T(8,128)(2,1)} %q_hbm.1, bf16[256,512]{1,0:T(8,128)(2,1)} %k_hbm.1, bf16[256,512]{1,0:T(8,128)(2,1)} %v_hbm.1, ...), custom_call_target="tpu_custom_call" | custom-call | tf_op jit(solution)/shard_map/exchange/pallas_call | solution.py:254
  44.0 1.4 %finish.1 = (bf16[256,512]{1,0:T(8,128)(2,1)}, bf16[256,512]{1,0:T(8,128)(2,1)}, bf16[256,512]{1,0:T(8,128)(2,1)}, bf16[256,512]{1,0:T(8,128)(2,1)}) custom-call(bf16[256,8,128]{2,1,0:T(8,128)(2,1)S(1)} %get-tuple-element.9.o_ref, bf16[2,128,4,128]{3,2,1,0:T(4,128)(2,1)S(1)} %get-tuple-element.10.d_ref, bf16[256,512]{1,0:T(8,128)(2,1)S(1)} %get-tuple-element.11.c_ref, ...), custom_call_target="tpu_custom_call" | custom-call | tf_op jit(solution)/shard_map/finish/pallas_call | solution.py:286

commit v5 on v4

--- a/solution.py
+++ b/solution.py
@@ -176,6 +176,16 @@
                 acc[1] += si
             spec[2 * n + i, 0], spec[2 * n + i, 1], spec[2 * n + i, 2], spec[2 * n + i, 3] = gr, gi, dr, di
 
+    def halves(kinds, send):
+        for h in range(2):
+            for x, y in sorted(((x, y) for y in range(4) for x in range(4)), key=lambda p: min(p[0], 2) + min(p[1], 2)):
+                for kind in kinds:
+                    c = y * 8 + h * 4 + x
+                    if kind:
+                        send(c, kind)
+                    else:
+                        pl.when(me != c)(lambda c=c, kind=kind: send(c, kind))
+
     def results(n):
         hr, hi = acc[2], acc[3]
         parts = []
@@ -189,10 +199,11 @@
             osnd[2 * n + i] = y.astype(BF16).reshape(CTX, 8, R)
         if n == 0:
             pltpu.make_async_copy(osnd.at[0, me], out_ref.at[mine], r_out.at[0]).start()
-        for c in all_cs:
-            for i, t in enumerate(sources(n)):
-                if c is not me or n or i:
-                    remote(osnd.at[2 * n + i, c], out_ref.at[mine], s_out.at[0], r_out.at[0], c, t).start()
+        def send(c, kind):
+            i = kind - 2 * n
+            remote(osnd.at[kind, c], out_ref.at[mine], s_out.at[0], r_out.at[0], c, sources(n)[i]).start()
+
+        halves((2 * n, 2 * n + 1), send)
 
     def filter_gradient():
         u = dot(pack(acc[0], acc[1]), fi[...])
@@ -200,10 +211,7 @@
         csnd[...] = total.astype(BF16).reshape(CTX, Q, R)
         place = fil_ref.at[core, me * 4 + zlo]
         pltpu.make_async_copy(csnd.at[me], place, r_c.at[0]).start()
-        for c in all_cs:
-            for i, t in enumerate(chips):
-                if c is not me or i:
-                    remote(csnd.at[c], place, s_c.at[0], r_c.at[0], c, t).start()
+        halves(range(4), lambda c, i: remote(csnd.at[c], place, s_c.at[0], r_c.at[0], c, chips[i]).start())
 
     analyse(0)
     drain(frcv, r_f.at[0])

time: 45.5 us -> 45 us (0.989)
  Pallas kernels: 44.8 us -> 44.2 us
    pallas_call x1, Pallas kernels: 43.4 us -> 42.9 us  [per_device(): pl.pallas_call(exchange_kernel, out_shape=(jax.ShapeDtypeStruct((FILTERS,...]
where the time goes in v5:
time: 45 us; the launch traced here: 44.9 us
  Pallas kernels  44.2 us (98%)
  between operations  0.64 us (1%)
    pallas_call x1, Pallas kernels, per_device(): pl.pallas_call(exchange_kernel, out_shape=(jax.ShapeDtypeStruct((FILTERS,...  42.9 us
    pallas_call x1, Pallas kernels, per_device(): pl.pallas_call(finish_kernel, out_shape=(block,) * 4, in_specs=[vmem] * 5...  1.38 us

profile of v5, /device:TPU:1, one launch (start us, length us, event | category | flops | bytes accessed | tf_op | source)
XLA Modules:
  0.0 44.9 jit_solution(2675879742176447219)
XLA Ops:
  0.6 42.9 %exchange.1 = (bf16[256,8,128]{2,1,0:T(8,128)(2,1)S(1)}, bf16[2,128,4,128]{3,2,1,0:T(4,128)(2,1)S(1)}, bf16[256,512]{1,0:T(8,128)(2,1)S(1)}, bf16[256,512]{1,0:T(8,128)(2,1)S(1)}, bf16[256,512]{1,0:T(8,128)(2,1)S(1)}) custom-call(bf16[256,512]{1,0:T(8,128)(2,1)} %q_hbm.1, bf16[256,512]{1,0:T(8,128)(2,1)} %k_hbm.1, bf16[256,512]{1,0:T(8,128)(2,1)} %v_hbm.1, ...), custom_call_target="tpu_custom_call" | custom-call | tf_op jit(solution)/shard_map/exchange/pallas_call | solution.py:262
  43.5 1.4 %finish.1 = (bf16[256,512]{1,0:T(8,128)(2,1)}, bf16[256,512]{1,0:T(8,128)(2,1)}, bf16[256,512]{1,0:T(8,128)(2,1)}, bf16[256,512]{1,0:T(8,128)(2,1)}) custom-call(bf16[256,8,128]{2,1,0:T(8,128)(2,1)S(1)} %get-tuple-element.9.o_ref, bf16[2,128,4,128]{3,2,1,0:T(4,128)(2,1)S(1)} %get-tuple-element.10.d_ref, bf16[256,512]{1,0:T(8,128)(2,1)S(1)} %get-tuple-element.11.c_ref, ...), custom_call_target="tpu_custom_call" | custom-call | tf_op jit(solution)/shard_map/finish/pallas_call | solution.py:294

commit v6 on v5

--- a/solution.py
+++ b/solution.py
@@ -115,12 +115,22 @@
     for t in chips[1:]:
         pl.semaphore_signal(known, inc=1, device_id=(me, t), device_id_type=MESH)
 
+    late = sorted((y * 8 + x for y in range(4) for x in range(4)), key=lambda p: -min(p % 8, 2) - min(p // 8, 2))
+
     def send_in(n):
-        for c in all_cs:
-            for i, (dz, dk) in enumerate(sets[n]):
-                if c is not me or dz or dk:
+        for h in (1, 0):
+            for j in range(16):
+                for i, (dz, dk) in enumerate(sets[n]):
                     t = beside(dz, dk)
-                    remote(snd.at[c * TP + t], rcv.at[tp, me], s_in.at[0], r_in.at[n, i], c, t).start()
+                    c = late[j] + 4 * h if n > 0 else (far if h else near)[j]
+
+                    def send(c=c, t=t, i=i):
+                        remote(snd.at[c * TP + t], rcv.at[tp, me], s_in.at[0], r_in.at[n, i], c, t).start()
+
+                    if j or dz or dk:
+                        send()
+                    elif h:
+                        send()
 
     pltpu.make_async_copy(snd.at[mine], rcv.at[tp, me], r_in.at[0, 0]).start()
     send_in(0)

time: 45 us -> 44.5 us (0.989)
  Pallas kernels: 44.2 us -> 43.7 us
    pallas_call x1, Pallas kernels: 42.9 us -> 42.4 us  [per_device(): pl.pallas_call(exchange_kernel, out_shape=(jax.ShapeDtypeStruct((FILTERS,...]
where the time goes in v6:
time: 44.5 us; the launch traced here: 44.4 us
  Pallas kernels  43.7 us (98%)
  between operations  0.64 us (1%)
    pallas_call x1, Pallas kernels, per_device(): pl.pallas_call(exchange_kernel, out_shape=(jax.ShapeDtypeStruct((FILTERS,...  42.4 us
    pallas_call x1, Pallas kernels, per_device(): pl.pallas_call(finish_kernel, out_shape=(block,) * 4, in_specs=[vmem] * 5...  1.38 us

profile of v6, /device:TPU:1, one launch (start us, length us, event | category | flops | bytes accessed | tf_op | source)
XLA Modules:
  0.0 44.4 jit_solution(16943253551470731538)
XLA Ops:
  0.6 42.4 %exchange.1 = (bf16[256,8,128]{2,1,0:T(8,128)(2,1)S(1)}, bf16[2,128,4,128]{3,2,1,0:T(4,128)(2,1)S(1)}, bf16[256,512]{1,0:T(8,128)(2,1)S(1)}, bf16[256,512]{1,0:T(8,128)(2,1)S(1)}, bf16[256,512]{1,0:T(8,128)(2,1)S(1)}) custom-call(bf16[256,512]{1,0:T(8,128)(2,1)} %q_hbm.1, bf16[256,512]{1,0:T(8,128)(2,1)} %k_hbm.1, bf16[256,512]{1,0:T(8,128)(2,1)} %v_hbm.1, ...), custom_call_target="tpu_custom_call" | custom-call | tf_op jit(solution)/shard_map/exchange/pallas_call | solution.py:272
  43.0 1.4 %finish.1 = (bf16[256,512]{1,0:T(8,128)(2,1)}, bf16[256,512]{1,0:T(8,128)(2,1)}, bf16[256,512]{1,0:T(8,128)(2,1)}, bf16[256,512]{1,0:T(8,128)(2,1)}) custom-call(bf16[256,8,128]{2,1,0:T(8,128)(2,1)S(1)} %get-tuple-element.9.o_ref, bf16[2,128,4,128]{3,2,1,0:T(4,128)(2,1)S(1)} %get-tuple-element.10.d_ref, bf16[256,512]{1,0:T(8,128)(2,1)S(1)} %get-tuple-element.11.c_ref, ...), custom_call_target="tpu_custom_call" | custom-call | tf_op jit(solution)/shard_map/finish/pallas_call | solution.py:304

commit v7 on v6

--- a/solution.py
+++ b/solution.py
@@ -122,7 +122,7 @@
             for j in range(16):
                 for i, (dz, dk) in enumerate(sets[n]):
                     t = beside(dz, dk)
-                    c = late[j] + 4 * h if n > 0 else (far if h else near)[j]
+                    c = late[j] + 4 * h if n > 0 else (late[j] + zs[1] if h else near[j])
 
                     def send(c=c, t=t, i=i):
                         remote(snd.at[c * TP + t], rcv.at[tp, me], s_in.at[0], r_in.at[n, i], c, t).start()

time: 44.5 us -> 44.4 us (level)
  no operation moved by 1% of the time
where the time goes in v7:
time: 44.4 us; the launch traced here: 44.3 us
  Pallas kernels  43.7 us (98%)
  between operations  0.64 us (1%)
    pallas_call x1, Pallas kernels, per_device(): pl.pallas_call(exchange_kernel, out_shape=(jax.ShapeDtypeStruct((FILTERS,...  42.3 us
    pallas_call x1, Pallas kernels, per_device(): pl.pallas_call(finish_kernel, out_shape=(block,) * 4, in_specs=[vmem] * 5...  1.38 us

profile of v7, /device:TPU:1, one launch (start us, length us, event | category | flops | bytes accessed | tf_op | source)
XLA Modules:
  0.0 44.3 jit_solution(12722257537246971559)
XLA Ops:
  0.6 42.3 %exchange.1 = (bf16[256,8,128]{2,1,0:T(8,128)(2,1)S(1)}, bf16[2,128,4,128]{3,2,1,0:T(4,128)(2,1)S(1)}, bf16[256,512]{1,0:T(8,128)(2,1)S(1)}, bf16[256,512]{1,0:T(8,128)(2,1)S(1)}, bf16[256,512]{1,0:T(8,128)(2,1)S(1)}) custom-call(bf16[256,512]{1,0:T(8,128)(2,1)} %q_hbm.1, bf16[256,512]{1,0:T(8,128)(2,1)} %k_hbm.1, bf16[256,512]{1,0:T(8,128)(2,1)} %v_hbm.1, ...), custom_call_target="tpu_custom_call" | custom-call | tf_op jit(solution)/shard_map/exchange/pallas_call | solution.py:272
  42.9 1.4 %finish.1 = (bf16[256,512]{1,0:T(8,128)(2,1)}, bf16[256,512]{1,0:T(8,128)(2,1)}, bf16[256,512]{1,0:T(8,128)(2,1)}, bf16[256,512]{1,0:T(8,128)(2,1)}) custom-call(bf16[256,8,128]{2,1,0:T(8,128)(2,1)S(1)} %get-tuple-element.9.o_ref, bf16[2,128,4,128]{3,2,1,0:T(4,128)(2,1)S(1)} %get-tuple-element.10.d_ref, bf16[256,512]{1,0:T(8,128)(2,1)S(1)} %get-tuple-element.11.c_ref, ...), custom_call_target="tpu_custom_call" | custom-call | tf_op jit(solution)/shard_map/finish/pallas_call | solution.py:304
